TPU v7x, 32 devices: a whole 2x2x4 slice. The times are simulated.
32 devices in a mesh: group: 4 (over y, core), member: 8 (over z, x).
Axes of the slice: x: 2, y: 2, z: 4, core: 2. Of those that a mesh axis runs over, the one named last changes fastest.
Arguments:
- volume_frac: float32 [256, 512, 256], P('group', 'member'), may hold values from 0 to 1
- velocity: bfloat16 [3, 256, 512, 256], P(None, 'group', 'member'), may hold values from -6 to 6
- drop_block: int32 [4, 8, 16], P('group', 'member'), may hold values from 0 to 255, as said below
- drop_owner: int32 [4, 8, 16, 1], P('group', 'member'), may hold values from 0 to 7; in each aligned block of 16 rows (0 to 15, 16 to 31, ..., all dimensions but the last counted through in order) at most 2 rows name the same one
- parcel_vel: float32 [4, 8, 8, 2, 3, 512], P('group', 'member'), may hold values from -6 to 6
- parcel_rate: float32 [4, 8, 8, 2, 512], P('group', 'member'), may hold values from 0.05 to 0.8
- parcel_weight: float32 [4, 8, 8, 2, 512], P('group', 'member'), may hold values from 0.3 to 3
- parcel_cell: int32 [4, 8, 8, 2, 512], P('group', 'member'), may hold values from 0 to 4095
Outputs:
- frac_next: float32 [256, 512, 256], P('group', 'member')
- velocity_next: bfloat16 [3, 256, 512, 256], P(None, 'group', 'member')
- parcel_next: float32 [4, 8, 8, 2, 3, 512], P('group', 'member')
Inputs may be any that keep to these rules, and one draw needn't show every extreme that they name: `drop_block`: the 16 entries of one device are distinct. `drop_owner`: no owner gets more than 2 of one device's droplet blocks; some device sends exactly 2 to one owner.
All inputs are finite; a program needn't handle non-finite values.
Results may differ from a plain program's by a relative error of at most 0.001.
Values may be sent and summed in bfloat16 or wider, within the bound.
No kernel may reach another device: no remote copies, remote signals or barrier semaphores. Data moves between devices by JAX's collectives and lax.ppermute only.
A program may use at most 448 MiB of HBM per device.

v0:
```python
import jax
import jax.numpy as jnp
from jax import lax
from jax.sharding import PartitionSpec as P

CAP = 2


courant = 0.025


def passed_along(block, axis, distance):
    devices = range(lax.axis_size(axis))
    route = [(i - distance, i) for i in devices if i - distance in devices]
    return lax.ppermute(block, axis, route)


def upwind_div(frac_ext, speed_low, along):
    count = frac_ext.shape[along]
    lower_frac = lax.slice_in_dim(frac_ext, 0, count - 1, axis=along)
    upper_frac = lax.slice_in_dim(frac_ext, 1, count, axis=along)
    face_flux = courant * (
        jnp.maximum(speed_low, 0.0) * lower_frac + jnp.minimum(speed_low, 0.0) * upper_frac
    )
    length = face_flux.shape[along]
    return lax.slice_in_dim(face_flux, 1, length, axis=along) - lax.slice_in_dim(
        face_flux, 0, length - 1, axis=along
    )


def one_slot(block_data, filled, parcel_v, drag_rate, weight, cell_ids):
    onehot = (cell_ids[:, None] == lax.iota(jnp.int32, 4096)[None, :]).astype(jnp.bfloat16)
    sampled = jnp.einsum("kc,pc->kp", block_data, onehot, preferred_element_type=jnp.float32)
    gas_share = 1.0 - sampled[3]
    acceleration = filled.astype(jnp.float32) * drag_rate * gas_share * (sampled[:3] - parcel_v)
    deposit_w = (weight * acceleration).astype(jnp.bfloat16)
    source = jnp.einsum("kp,pc->kc", deposit_w, onehot, preferred_element_type=jnp.float32)
    return (parcel_v + acceleration, source.astype(jnp.bfloat16))


def spray_work(block_data, filled, parcel_v, drag_rate, weight, cell_ids):
    slot_count = block_data.shape[0]
    batched = (block_data, filled, parcel_v, drag_rate, weight, cell_ids)
    batched = jax.tree.map(
        lambda item: item.reshape((slot_count // 4, 4) + item.shape[1:]), batched
    )
    new_vel, source = lax.map(lambda group_items: jax.vmap(one_slot)(*group_items), batched)
    return (
        new_vel.reshape((slot_count,) + new_vel.shape[2:]),
        source.reshape((slot_count,) + source.shape[2:]),
    )


def block_corner(block_id, blocks_y, blocks_z):
    first = block_id // (blocks_y * blocks_z)
    second = block_id // blocks_z % blocks_y
    third = block_id % blocks_z
    return (first * 16, second * 16, third * 16)


def per_device(
    volume_frac,
    velocity,
    drop_block,
    drop_owner,
    parcel_vel,
    parcel_rate,
    parcel_weight,
    parcel_cell,
):
    members = lax.axis_size("member")
    cells_x, cells_y, cells_z = volume_frac.shape
    blocks_x = cells_x // 16
    blocks_y = cells_y // 16
    blocks_z = cells_z // 16
    block_total = blocks_x * blocks_y * blocks_z
    speed_first = velocity[0].astype(jnp.float32)
    speed_second = velocity[1].astype(jnp.float32)
    speed_third = velocity[2].astype(jnp.float32)
    below_first = passed_along(
        jnp.stack([volume_frac[-1], speed_first[-1]]).astype(jnp.bfloat16), "group", 1
    ).astype(jnp.float32)
    above_first = passed_along(volume_frac[:1].astype(jnp.bfloat16), "group", -1).astype(
        jnp.float32
    )
    below_second = passed_along(
        jnp.stack([volume_frac[:, -1], speed_second[:, -1]]).astype(jnp.bfloat16), "member", 1
    ).astype(jnp.float32)
    above_second = passed_along(volume_frac[:, :1].astype(jnp.bfloat16), "member", -1).astype(
        jnp.float32
    )
    frac_first = jnp.concatenate([below_first[0][None], volume_frac, above_first], 0)
    low_first = jnp.concatenate([below_first[1][None], speed_first], 0)
    frac_second = jnp.concatenate([below_second[0][:, None], volume_frac, above_second], 1)
    low_second = jnp.concatenate([below_second[1][:, None], speed_second], 1)
    frac_third = jnp.pad(volume_frac, ((0, 0), (0, 0), (1, 1)))
    low_third = jnp.pad(speed_third, ((0, 0), (0, 0), (1, 0)))
    change = (
        upwind_div(frac_first, low_first, 0)
        + upwind_div(frac_second, low_second, 1)
        + upwind_div(frac_third, low_third, 2)
    )
    frac_next = jnp.minimum(volume_frac - change, 1.0)
    block_ids = drop_block[0, 0]
    owners = drop_owner[0, 0, :, 0]
    drops = block_ids.shape[0]

    def fetch(block_id):
        first, second, third = block_corner(block_id, blocks_y, blocks_z)
        speeds = lax.dynamic_slice(velocity, (0, first, second, third), (3, 16, 16, 16)).reshape(
            3, 4096
        )
        fracs = lax.dynamic_slice(volume_frac, (first, second, third), (16, 16, 16)).reshape(
            1, 4096
        )
        return jnp.concatenate([speeds, fracs.astype(jnp.bfloat16)], 0)

    picked = jax.vmap(fetch)(block_ids)
    positions = lax.iota(jnp.int32, drops)
    earlier = positions[:, None] < positions[None, :]
    places = jnp.sum(((owners[:, None] == owners[None, :]) & earlier).astype(jnp.int32), axis=0)
    slot_of = owners * CAP + places
    slot_count = members * CAP
    chooser = (slot_of[None, :] == lax.iota(jnp.int32, slot_count)[:, None]).astype(jnp.bfloat16)
    outgoing = jnp.einsum(
        "sd,dkc->skc", chooser, picked, preferred_element_type=jnp.float32
    ).astype(jnp.bfloat16)
    filled = jnp.sum(chooser.astype(jnp.float32), axis=1).astype(jnp.bfloat16)
    parcels = parcel_vel.shape[-1]
    own_vel = parcel_vel[0, 0].reshape(slot_count, 3, parcels)
    own_rate = parcel_rate[0, 0].reshape(slot_count, parcels)
    own_weight = parcel_weight[0, 0].reshape(slot_count, parcels)
    own_cell = parcel_cell[0, 0].reshape(slot_count, parcels)
    received, flags_in = (
        lax.all_to_all(
            outgoing.reshape(members, CAP, 4, 4096),
            "member",
            split_axis=0,
            concat_axis=0,
            tiled=True,
        ),
        lax.all_to_all(
            filled.reshape(members, CAP), "member", split_axis=0, concat_axis=0, tiled=True
        ),
    )
    vel_out, source = spray_work(
        received.reshape(slot_count, 4, 4096),
        flags_in.reshape(slot_count),
        own_vel,
        own_rate,
        own_weight,
        own_cell,
    )
    returned = lax.all_to_all(
        source.reshape(members, CAP, 3, 4096), "member", split_axis=0, concat_axis=0, tiled=True
    ).reshape(slot_count, 3, 4096)
    block_hits = (block_ids[:, None] == lax.iota(jnp.int32, block_total)[None, :]).astype(
        jnp.bfloat16
    )
    placement = jnp.dot(chooser, block_hits, preferred_element_type=jnp.float32).astype(
        jnp.bfloat16
    )
    block_field = jnp.einsum("sb,skc->bkc", placement, returned, preferred_element_type=jnp.float32)
    block_field = block_field.reshape(blocks_x, blocks_y, blocks_z, 3, 16, 16, 16)
    drag_field = block_field.transpose(3, 0, 4, 1, 5, 2, 6).reshape(3, cells_x, cells_y, cells_z)
    velocity_next = (velocity.astype(jnp.float32) + drag_field).astype(jnp.bfloat16)
    parcel_next = vel_out.reshape(1, 1, members, CAP, 3, parcels)
    return (frac_next, velocity_next, parcel_next)


def solution(mesh):
    in_specs = (
        P("group", "member", None),
        P(None, "group", "member", None),
        P("group", "member", None),
        P("group", "member", None, None),
        P("group", "member", None, None, None, None),
        P("group", "member", None, None, None),
        P("group", "member", None, None, None),
        P("group", "member", None, None, None),
    )
    out_specs = (
        P("group", "member", None),
        P(None, "group", "member", None),
        P("group", "member", None, None, None, None),
    )
    return jax.shard_map(
        per_device, mesh=mesh, in_specs=in_specs, out_specs=out_specs, check_vma=False
    )
```

profile of v0, /device:TPU:6, one launch (start us, length us, event | category | flops | bytes accessed | tf_op | source)
XLA Modules:
  0.0 471.9 jit_solution(8264483617744455720)
XLA Ops:
  2.9 6.3 %all-to-all-start = ((bf16[8,1,2]{2,1,0:T(2,128)(2,1)}), bf16[8,1,2]{2,1,0:T(2,128)(2,1)S(1)}, u32[]{:S(2)}, u32[]{:S(2)}) async-start(bf16[8,1,2]{2,1,0:T(2,128)(2,1)} %all_to_all.16), calls=%async_computation | async-start | bytes 8192 | tf_op jit(solution)/shard_map/all_to_all | solution.py:142
  29.0 5.0 %collective-permute-start.2 = (bf16[2,64,256]{2,1,0:T(8,128)(2,1)}, bf16[2,64,256]{2,1,0:T(8,128)(2,1)S(1)}, u32[]{:S(2)}, u32[]{:S(2)}) collective-permute-start(bf16[2,64,256]{2,1,0:T(8,128)(2,1)} %pad_maximum_fusion.3), channel_id=1, source_target_pairs={{0,1},{1,2},{2,3},{3,4},{4,5},{5,6},{6,7},{8,9},{9,10},{10,11},{11... | collective-permute-start | bytes 196616 | tf_op jit(solution)/shard_map/ppermute | solution.py:15
  37.9 6.6 %copy.156 = f32[64,64,256]{2,0,1:T(8,128)} copy(f32[64,64,256]{2,1,0:T(8,128)} %param.10) | data formatting | bytes 8388608 | tf_op args[0]
  44.6 56.2 %while.16 = (s32[]{:T(128)}, bf16[64,64,256]{2,1,0:T(8,128)(2,1)}, s32[16,3]{0,1:T(4,128)S(1)}, bf16[16,16,16,16]{3,2,1,0:T(8,128)(2,1)S(1)}, s32[]{:T(128)}) while((s32[]{:T(128)}, bf16[64,64,256]{2,1,0:T(8,128)(2,1)}, s32[16,3]{0,1:T(4,128)S(1)}, bf16[16,16,16,16]{3,2,1,0:T(8,128)(2,1)S(1)}, s32[]{:T(128)}) %tuple.74), condition=%wide.while_cond.1, body=%wide.while_body.1.sunk | while | flops 2 | bytes 73865 | solution.py:113
  102.7 72.3 %while.15 = (s32[]{:T(128)}, bf16[3,64,64,256]{3,2,1,0:T(8,128)(2,1)}, s32[16,4]{0,1:T(4,128)S(1)}, bf16[16,3,16,16,16]{4,3,2,1,0:T(8,128)(2,1)}, s32[]{:T(128)}) while((s32[]{:T(128)}, bf16[3,64,64,256]{3,2,1,0:T(8,128)(2,1)}, s32[16,4]{0,1:T(4,128)S(1)}, bf16[16,3,16,16,16]{4,3,2,1,0:T(8,128)(2,1)}, s32[]{:T(128)}) %tuple.77), condition=%wide.while_cond, body=%wide.while_body.sunk | while | flops 2 | bytes 394885 | solution.py:110
  174.9 5.0 %reshape.371 = bf16[16,3,4096]{2,1,0:T(4,128)(2,1)S(1)} reshape(bf16[16,3,16,16,16]{4,3,2,1,0:T(8,128)(2,1)} %get-tuple-element.60) | data formatting | bytes 786432 | tf_op jit(solution)/shard_map/vmap()/reshape | solution.py:110
  180.5 6.2 %copy_bitcast_fusion.2 = (bf16[64,64,256]{2,0,1:T(8,128)(2,1)S(1)}, f32[64,64,256]{2,0,1:T(8,128)}) fusion(bf16[1,64,64,256]{3,2,1,0:T(8,128)(2,1)} %get-tuple-element.183, bf16[1,64,64,256]{3,2,1,0:T(8,128)(2,1)S(1)} %get-tuple-element.181), kind=kLoop, calls=%fused_computation.60 | loop fusion | flops 1048576 | bytes 10485760 | tf_op jit(solution)/shard_map/convert_element_type | solution.py:79
  193.9 4.9 %all-to-all-start.1 = ((bf16[8,2,4,4096]{3,1,2,0:T(2,128)(2,1)}), bf16[8,2,4,4096]{3,1,2,0:T(2,128)(2,1)S(1)}, u32[]{:S(2)}, u32[]{:S(2)}) async-start(bf16[8,2,4,4096]{3,1,2,0:T(2,128)(2,1)} %copy.160), calls=%async_computation.1 | async-start | bytes 1048576 | tf_op jit(solution)/shard_map/all_to_all | solution.py:135
  200.0 7.2 %fusion.24 = f32[64,65,256]{2,0,1:T(8,128)} fusion(f32[64,64,256]{2,0,1:T(8,128)} %copy.156, f32[64,1,256]{2,0,1:T(8,128)S(1)} %get-tuple-element.191, f32[64,1,256]{2,0,1:T(8,128)S(1)} %convert_element_type.96, f32[64,64,256]{2,0,1:T(8,128)} %get-tuple-element.186, f32[64,1,256]{2,0,1:T(8,128)S(1)} %get-tuple-element.190), kind=kLoop, calls=%fused_computation.51 | loop fusion | flops 9584640 | bytes 12845056 | tf_op jit(solution)/shard_map/mul | solution.py:22
  212.6 51.3 %while.14 = (s32[]{:T(128)}, f32[4,4,3,512]{3,2,1,0:T(4,128)S(1)}, bf16[4,4,3,4096]{3,2,1,0:T(4,128)(2,1)S(1)}, f32[4,4,3,512]{3,2,1,0:T(4,128)S(1)}, bf16[4,4]{...) while((s32[]{:T(128)}, f32[4,4,3,512]{3,2,1,0:T(4,128)S(1)}, ...), condition=%wide.region_3.4_spmd, body=%wide.region_2.3_spmd.sunk | while | flops 134316032 | bytes 591021 | solution.py:47
  212.7 6.3 %fusion.62 = f32[4,4,512]{2,1,0:T(4,128)S(1)} fusion(s32[4,512]{1,0:T(4,128)S(1)} %dynamic-slice_bitcast_fusion.4, bf16[4,4,4,4096]{3,2,1,0:T(4,128)(2,1)S(1)} %get-tuple-element.372, s32[]{:T(128)S(6)} %copy.225), kind=kOutput, calls=%fused_computation.2.clone.1 | convolution fusion | flops 75497472 | bytes 172036 | tf_op jit(solution)/shard_map/while/body/eval_jaxpr/vmap(kc,pc->kp)/dot_general | solution.py:33
  219.0 6.4 %fusion.65 = bf16[4,4,3,4096]{3,2,1,0:T(4,128)(2,1)S(1)} fusion(bf16[4,4,3,4096]{3,2,1,0:T(4,128)(2,1)S(1)} %get-tuple-element.358, s32[]{:T(128)S(6)} %copy.225, s32[4,512]{1,0:T(4,128)S(1)} %dynamic-slice_bitcast_fusion.4, f32[4,512]{1,0:T(4,128)S(1)} %dynamic-slice_bitcast_fusion.5, f32[4,4,512]{2,1,0:T(4,128)S(1)} %fusion.62, ...), kind=kOutput, calls=%fused_computation.7.clone.1 | convolution fusion | flops 58793984 | bytes 222208 | tf_op jit(solution)/shard_map/while/body/eval_jaxpr/vmap(kp,pc->kc)/dot_general | solution.py:37
  225.5 6.3 %fusion.62 = f32[4,4,512]{2,1,0:T(4,128)S(1)} fusion(s32[4,512]{1,0:T(4,128)S(1)} %dynamic-slice_bitcast_fusion.4, bf16[4,4,4,4096]{3,2,1,0:T(4,128)(2,1)S(1)} %get-tuple-element.372, s32[]{:T(128)S(6)} %copy.225), kind=kOutput, calls=%fused_computation.2.clone.1 | convolution fusion | flops 75497472 | bytes 172036 | tf_op jit(solution)/shard_map/while/body/eval_jaxpr/vmap(kc,pc->kp)/dot_general | solution.py:33
  231.9 6.4 %fusion.65 = bf16[4,4,3,4096]{3,2,1,0:T(4,128)(2,1)S(1)} fusion(bf16[4,4,3,4096]{3,2,1,0:T(4,128)(2,1)S(1)} %get-tuple-element.358, s32[]{:T(128)S(6)} %copy.225, s32[4,512]{1,0:T(4,128)S(1)} %dynamic-slice_bitcast_fusion.4, f32[4,512]{1,0:T(4,128)S(1)} %dynamic-slice_bitcast_fusion.5, f32[4,4,512]{2,1,0:T(4,128)S(1)} %fusion.62, ...), kind=kOutput, calls=%fused_computation.7.clone.1 | convolution fusion | flops 58793984 | bytes 222208 | tf_op jit(solution)/shard_map/while/body/eval_jaxpr/vmap(kp,pc->kc)/dot_general | solution.py:37
  238.3 6.3 %fusion.62 = f32[4,4,512]{2,1,0:T(4,128)S(1)} fusion(s32[4,512]{1,0:T(4,128)S(1)} %dynamic-slice_bitcast_fusion.4, bf16[4,4,4,4096]{3,2,1,0:T(4,128)(2,1)S(1)} %get-tuple-element.372, s32[]{:T(128)S(6)} %copy.225), kind=kOutput, calls=%fused_computation.2.clone.1 | convolution fusion | flops 75497472 | bytes 172036 | tf_op jit(solution)/shard_map/while/body/eval_jaxpr/vmap(kc,pc->kp)/dot_general | solution.py:33
  244.7 6.4 %fusion.65 = bf16[4,4,3,4096]{3,2,1,0:T(4,128)(2,1)S(1)} fusion(bf16[4,4,3,4096]{3,2,1,0:T(4,128)(2,1)S(1)} %get-tuple-element.358, s32[]{:T(128)S(6)} %copy.225, s32[4,512]{1,0:T(4,128)S(1)} %dynamic-slice_bitcast_fusion.4, f32[4,512]{1,0:T(4,128)S(1)} %dynamic-slice_bitcast_fusion.5, f32[4,4,512]{2,1,0:T(4,128)S(1)} %fusion.62, ...), kind=kOutput, calls=%fused_computation.7.clone.1 | convolution fusion | flops 58793984 | bytes 222208 | tf_op jit(solution)/shard_map/while/body/eval_jaxpr/vmap(kp,pc->kc)/dot_general | solution.py:37
  251.1 6.3 %fusion.62 = f32[4,4,512]{2,1,0:T(4,128)S(1)} fusion(s32[4,512]{1,0:T(4,128)S(1)} %dynamic-slice_bitcast_fusion.4, bf16[4,4,4,4096]{3,2,1,0:T(4,128)(2,1)S(1)} %get-tuple-element.372, s32[]{:T(128)S(6)} %copy.225), kind=kOutput, calls=%fused_computation.2.clone.1 | convolution fusion | flops 75497472 | bytes 172036 | tf_op jit(solution)/shard_map/while/body/eval_jaxpr/vmap(kc,pc->kp)/dot_general | solution.py:33
  257.5 6.4 %fusion.65 = bf16[4,4,3,4096]{3,2,1,0:T(4,128)(2,1)S(1)} fusion(bf16[4,4,3,4096]{3,2,1,0:T(4,128)(2,1)S(1)} %get-tuple-element.358, s32[]{:T(128)S(6)} %copy.225, s32[4,512]{1,0:T(4,128)S(1)} %dynamic-slice_bitcast_fusion.4, f32[4,512]{1,0:T(4,128)S(1)} %dynamic-slice_bitcast_fusion.5, f32[4,4,512]{2,1,0:T(4,128)S(1)} %fusion.62, ...), kind=kOutput, calls=%fused_computation.7.clone.1 | convolution fusion | flops 58793984 | bytes 222208 | tf_op jit(solution)/shard_map/while/body/eval_jaxpr/vmap(kp,pc->kc)/dot_general | solution.py:37
  265.1 6.3 %all-to-all-start.2 = ((bf16[8,2,3,4096]{3,1,2,0:T(2,128)(2,1)}), bf16[8,2,3,4096]{3,1,2,0:T(2,128)(2,1)S(1)}, u32[]{:S(2)}, u32[]{:S(2)}) async-start(bf16[8,2,3,4096]{3,1,2,0:T(2,128)(2,1)} %copy.164), calls=%async_computation.2 | async-start | bytes 786432 | tf_op jit(solution)/shard_map/all_to_all | solution.py:154
  271.4 12.9 %fusion.27 = f32[64,64,256]{2,0,1:T(8,128)S(1)} fusion(f32[64,64,257]{2,0,1:T(8,128)} %fusion.19, f32[64,65,256]{2,0,1:T(8,128)} %fusion.24, f32[65,64,256]{2,0,1:T(8,128)} %fusion.22, f32[64,64,256]{2,1,0:T(8,128)} %param.10), kind=kLoop, calls=%fused_computation.56 | loop fusion | flops 7340032 | bytes 33554432 | tf_op jit(solution)/shard_map/min | solution.py:103
  291.5 35.3 %convolution_bitcast_fusion = f32[3,4,16,4,16,16,16]{6,5,4,2,0,3,1:T(8,128)} fusion(bf16[4,4,16,16,1,1,1]{3,2,6,5,4,1,0:T(8,128)(2,1)} %bitcast.172, bf16[3,16,16,16,16,1,1]{4,3,2,1,0,6,5:T(8,128)(2,1)S(1)} %bitcast.165), kind=kOutput, calls=%fused_computation.32 | convolution fusion | flops 100663296 | bytes 12984320 | tf_op jit(solution)/shard_map/sb,skc->bkc/dot_general | solution.py:163
  326.8 64.8 %copy.168 = f32[3,4,16,4,16,16,16]{6,5,4,3,2,1,0:T(8,128)} copy(f32[3,4,16,4,16,16,16]{6,5,4,2,0,3,1:T(8,128)} %convolution_bitcast_fusion) | data formatting | bytes 25165824 | tf_op jit(solution)/shard_map/transpose | solution.py:165
  391.7 68.0 %reshape.315 = f32[3,64,64,256]{3,2,1,0:T(8,128)} reshape(f32[3,4,16,4,16,16,16]{6,5,4,3,2,1,0:T(8,128)} %copy.168) | data formatting | bytes 25165824 | tf_op jit(solution)/shard_map/reshape | solution.py:165
  459.7 11.8 %add_convert_fusion = bf16[3,64,64,256]{3,2,1,0:T(8,128)(2,1)} fusion(f32[3,64,64,256]{3,2,1,0:T(8,128)} %reshape.315, bf16[3,64,64,256]{3,2,1,0:T(8,128)(2,1)} %get-tuple-element.376), kind=kLoop, calls=%fused_computation.33 | loop fusion | flops 9437184 | bytes 25165824 | tf_op jit(solution)/shard_map/convert_element_type | solution.py:166
  (202 shorter events, 179.3 us)
Async XLA Ops:
  2.9 191.0 %all-to-all-start = ((bf16[8,1,2]{2,1,0:T(2,128)(2,1)}), bf16[8,1,2]{2,1,0:T(2,128)(2,1)S(1)}, u32[]{:S(2)}, u32[]{:S(2)}) async-start(bf16[8,1,2]{2,1,0:T(2,128)(2,1)} %all_to_all.16), calls=%async_computation | async-start | bytes 8192 | tf_op jit(solution)/shard_map/all_to_all | solution.py:142
  9.2 7.8 %copy-start.2 = (bf16[3,64,64,256]{3,2,1,0:T(8,128)(2,1)S(1)}, bf16[3,64,64,256]{3,2,1,0:T(8,128)(2,1)}, u32[]{:S(2)}) copy-start(bf16[3,64,64,256]{3,2,1,0:T(8,128)(2,1)} %param.11) | copy-start | bytes 18874372
  14.4 184.5 %collective-permute-start.3 = (bf16[64,1,256]{2,0,1:T(8,128)(2,1)}, bf16[64,1,256]{2,0,1:T(8,128)(2,1)}, u32[]{:S(2)}, u32[]{:S(2)}) collective-permute-start(bf16[64,1,256]{2,0,1:T(8,128)(2,1)} %get-tuple-element.188), channel_id=1, source_target_pairs={{1,0},{2,1},{3,2},{4,3},{5,4},{6,5},{7,6},{9,8},{10,9},{11,10},{12... | collective-permute-start | bytes 98312 | tf_op jit(solution)/shard_map/ppermute | solution.py:15
  17.3 182.6 %collective-permute-start = (bf16[2,64,256]{2,0,1:T(2,128)(2,1)S(1)}, bf16[2,64,256]{2,0,1:T(2,128)(2,1)S(1)}, u32[]{:S(2)}, u32[]{:S(2)}) collective-permute-start(bf16[2,64,256]{2,0,1:T(2,128)(2,1)S(1)} %pad_maximum_fusion.2), channel_id=1, source_target_pairs={{0,8},{8,16},{16,24},{1,9},{9,17},{17,25},{2,10},{10,18},{18,26},{... | collective-permute-start | bytes 196616 | tf_op jit(solution)/shard_map/ppermute | solution.py:15
  19.2 180.5 %collective-permute-start.1 = (bf16[1,64,256]{2,0,1:T(2,128)(2,1)}, bf16[1,64,256]{2,0,1:T(2,128)(2,1)S(1)}, u32[]{:S(2)}, u32[]{:S(2)}) collective-permute-start(bf16[1,64,256]{2,0,1:T(2,128)(2,1)} %get-tuple-element.184), channel_id=1, source_target_pairs={{8,0},{16,8},{24,16},{9,1},{17,9},{25,17},{10,2},{18,10},{26,18},{... | collective-permute-start | bytes 98312 | tf_op jit(solution)/shard_map/ppermute | solution.py:15
  29.0 170.8 %collective-permute-start.2 = (bf16[2,64,256]{2,1,0:T(8,128)(2,1)}, bf16[2,64,256]{2,1,0:T(8,128)(2,1)S(1)}, u32[]{:S(2)}, u32[]{:S(2)}) collective-permute-start(bf16[2,64,256]{2,1,0:T(8,128)(2,1)} %pad_maximum_fusion.3), channel_id=1, source_target_pairs={{0,1},{1,2},{2,3},{3,4},{4,5},{5,6},{6,7},{8,9},{9,10},{10,11},{11... | collective-permute-start | bytes 196616 | tf_op jit(solution)/shard_map/ppermute | solution.py:15
  37.9 6.6 %copy-start.8 = (s32[1,1,16]{2,1,0:T(1,128)S(1)}, s32[1,1,16]{2,1,0:T(1,128)}, u32[]{:S(2)}) copy-start(s32[1,1,16]{2,1,0:T(1,128)} %param.12) | copy-start | bytes 196
  180.5 6.2 %copy-start = (f32[64,64,256]{2,0,1:T(8,128)S(1)}, f32[64,64,256]{2,0,1:T(8,128)}, u32[]{:S(2)}) copy-start(f32[64,64,256]{2,0,1:T(8,128)} %copy.156) | copy-start | bytes 12582916
  186.7 4.7 %copy-start.5 = (f32[1,1,8,2,512]{4,3,2,1,0:T(2,128)S(1)}, f32[1,1,8,2,512]{4,3,2,1,0:T(2,128)}, u32[]{:S(2)}) copy-start(f32[1,1,8,2,512]{4,3,2,1,0:T(2,128)} %param.15) | copy-start | bytes 98308
  186.7 4.8 %copy-start.6 = (f32[1,1,8,2,512]{4,3,2,1,0:T(2,128)S(1)}, f32[1,1,8,2,512]{4,3,2,1,0:T(2,128)}, u32[]{:S(2)}) copy-start(f32[1,1,8,2,512]{4,3,2,1,0:T(2,128)} %param.16) | copy-start | bytes 98308
  186.7 4.8 %copy-start.7 = (s32[1,1,8,2,512]{4,3,2,1,0:T(2,128)S(1)}, s32[1,1,8,2,512]{4,3,2,1,0:T(2,128)}, u32[]{:S(2)}) copy-start(s32[1,1,8,2,512]{4,3,2,1,0:T(2,128)} %param.17) | copy-start | bytes 98308
  186.7 5.6 %copy-start.4 = (f32[1,1,8,2,3,512]{5,3,4,2,1,0:T(2,128)S(1)}, f32[1,1,8,2,3,512]{5,3,4,2,1,0:T(2,128)}, u32[]{:S(2)}) copy-start(f32[1,1,8,2,3,512]{5,3,4,2,1,0:T(2,128)} %param.14) | copy-start | bytes 294916
  193.9 18.2 %all-to-all-start.1 = ((bf16[8,2,4,4096]{3,1,2,0:T(2,128)(2,1)}), bf16[8,2,4,4096]{3,1,2,0:T(2,128)(2,1)S(1)}, u32[]{:S(2)}, u32[]{:S(2)}) async-start(bf16[8,2,4,4096]{3,1,2,0:T(2,128)(2,1)} %copy.160), calls=%async_computation.1 | async-start | bytes 1048576 | tf_op jit(solution)/shard_map/all_to_all | solution.py:135
  200.0 7.2 %copy-start.1 = (f32[64,64,256]{2,0,1:T(8,128)S(1)}, f32[64,64,256]{2,0,1:T(8,128)}, u32[]{:S(2)}) copy-start(f32[64,64,256]{2,0,1:T(8,128)} %copy.156) | copy-start | bytes 12582916
  200.0 8.7 %copy-start.3 = (f32[64,64,256]{2,0,1:T(8,128)S(1)}, f32[64,64,256]{2,0,1:T(8,128)}, u32[]{:S(2)}) copy-start(f32[64,64,256]{2,0,1:T(8,128)} %get-tuple-element.198) | copy-start | bytes 12582916
  265.1 24.4 %all-to-all-start.2 = ((bf16[8,2,3,4096]{3,1,2,0:T(2,128)(2,1)}), bf16[8,2,3,4096]{3,1,2,0:T(2,128)(2,1)S(1)}, u32[]{:S(2)}, u32[]{:S(2)}) async-start(bf16[8,2,3,4096]{3,1,2,0:T(2,128)(2,1)} %copy.164), calls=%async_computation.2 | async-start | bytes 786432 | tf_op jit(solution)/shard_map/all_to_all | solution.py:154
where the time goes:
time: 480 us; the launch traced here: 472 us
  local copies, waits for them, and re-layouts  297 us (62%)
  matrix products  86.3 us (18%)
  other arithmetic  57 us (12%)
  starting transfers between devices  30 us (6%)
    gather x96, local copies, waits for them, and re-layouts  128 us
    reshape x1, local copies, waits for them, and re-layouts, per_device(): block_field.transpose(3, 0, 4, 1, 5, 2, 6)  68 us
    transpose x1, local copies, waits for them, and re-layouts, per_device(): block_field.transpose(3, 0, 4, 1, 5, 2, 6)  64.8 us
    dot_general x1, matrix products, per_device(): jnp.einsum('sb,skc->bkc', placement, returned, preferred_element_type=jnp...  35.3 us
    dot_general x4, matrix products, one_slot(): jnp.einsum('kp,pc->kc', deposit_w, onehot, preferred_element_type=jnp.flo...  25.5 us
    dot_general x4, matrix products, one_slot(): jnp.einsum('kc,pc->kp', block_data, onehot, preferred_element_type=jnp.fl...  25.1 us
    unnamed x23, local copies, waits for them, and re-layouts  17.9 us
    mul x3, other arithmetic, upwind_div(): courant * (jnp.maximum(speed_low, 0.0) * lower_frac + jnp.minimum(speed_l...  15.2 us
  transfers between devices with their start and end apart: 7, of which 0 were waited for; matrix products, arithmetic and copies ran while one was open for 43% of the time, Pallas kernels for 0%

commit v1 on v0

v1 whole, which is shorter than its diff:
```python
import functools

import jax
import jax.numpy as jnp
from jax import lax
from jax.experimental import pallas as pl
from jax.experimental.pallas import tpu as pltpu
from jax.sharding import PartitionSpec as P

CAP = 2
EDGE = 16
LANES = 128
FIELDS = 6

courant = 0.025

F32 = jnp.float32
BF16 = jnp.bfloat16


def passed_along(block, axis, distance):
    devices = range(lax.axis_size(axis))
    route = [(i - distance, i) for i in devices if i - distance in devices]
    return lax.ppermute(block, axis, route)


def whole(shape):
    return pl.BlockSpec(shape, lambda *_: (0,) * len(shape))


def params(**more):
    return pltpu.CompilerParams(vmem_limit_bytes=56 * 1024 * 1024, **more)


def pack_body(
    vel_ref, rate_ref, weight_ref, cell_ref,
    f_first_x, f_last_x, u_last_x, f_first_y, f_last_y, u_last_y,
    parcels_ref, up_x, down_x, up_y, down_y,
):
    parcels_ref[:, 0:3] = vel_ref[...]
    parcels_ref[:, 3] = rate_ref[...]
    parcels_ref[:, 4] = weight_ref[...]
    parcels_ref[:, 5] = cell_ref[...].astype(F32)
    up_x[0] = f_last_x[0].astype(BF16)
    up_x[1] = u_last_x[0, 0]
    down_x[0] = f_first_x[0].astype(BF16)
    up_y[0] = f_last_y[:, 7, :].astype(BF16)
    up_y[1] = u_last_y[0].astype(F32)[:, 15, :].astype(BF16)
    down_y[0] = f_first_y[:, 0, :].astype(BF16)


def pack(volume_frac, velocity, vel, rate, weight, cell):
    nx, ny, nz = volume_frac.shape
    members, _, parcels = rate.shape
    return pl.pallas_call(
        pack_body,
        grid=(1,),
        in_specs=[
            whole(vel.shape),
            whole(rate.shape),
            whole(weight.shape),
            whole(cell.shape),
            pl.BlockSpec((1, ny, nz), lambda i: (0, 0, 0)),
            pl.BlockSpec((1, ny, nz), lambda i: (nx - 1, 0, 0)),
            pl.BlockSpec((1, 1, ny, nz), lambda i: (0, nx - 1, 0, 0)),
            pl.BlockSpec((nx, 8, nz), lambda i: (0, 0, 0)),
            pl.BlockSpec((nx, 8, nz), lambda i: (0, ny // 8 - 1, 0)),
            pl.BlockSpec((1, nx, 16, nz), lambda i: (1, 0, ny // 16 - 1, 0)),
        ],
        out_specs=[
            whole((members, FIELDS, CAP, parcels)),
            whole((2, ny, nz)),
            whole((1, ny, nz)),
            whole((2, nx, nz)),
            whole((1, nx, nz)),
        ],
        out_shape=[
            jax.ShapeDtypeStruct((members, FIELDS, CAP, parcels), F32),
            jax.ShapeDtypeStruct((2, ny, nz), BF16),
            jax.ShapeDtypeStruct((1, ny, nz), BF16),
            jax.ShapeDtypeStruct((2, nx, nz), BF16),
            jax.ShapeDtypeStruct((1, nx, nz), BF16),
        ],
        compiler_params=params(),
        name="pack",
    )(
        vel, rate, weight, cell,
        volume_frac, volume_frac, velocity, volume_frac, volume_frac, velocity,
    )


def slot_table(block_sm, owner_sm, table, count, drops, members):
    def clear_count(i, _):
        count[i] = 0
        return 0

    def clear_table(i, _):
        table[i] = -1
        return 0

    lax.fori_loop(0, members, clear_count, 0)
    lax.fori_loop(0, members * CAP, clear_table, 0)

    def enter(j, _):
        owner = owner_sm[j]
        place = count[owner]
        count[owner] = place + 1
        table[owner * CAP + place] = block_sm[j]
        return 0

    lax.fori_loop(0, drops, enter, 0)


def rows_of_cell(cell):
    high = lax.shift_right_logical(cell, 4)
    rows = lax.broadcasted_iota(jnp.int32, (EDGE * EDGE, cell.shape[-1]), 0)
    return jnp.where(rows == high, 1.0, 0.0).astype(BF16)


def sample_body(
    blocks_y, blocks_z, block_sm, owner_sm, parcels_ref, frac_hbm, velocity_hbm, out_ref,
    speeds, fracs, table, count, sems,
):
    members = parcels_ref.shape[0]
    drops = block_sm.shape[0]
    slot_table(block_sm, owner_sm, table, count, drops, members)

    def copies(slot):
        block = jnp.maximum(table[slot], 0)
        bx = block // (blocks_y * blocks_z)
        by = block // blocks_z % blocks_y
        bz = block % blocks_z
        x = bx * EDGE
        y = pl.multiple_of(by * EDGE, EDGE)
        z = pl.multiple_of(bz * EDGE // LANES * LANES, LANES)
        return (
            pltpu.make_async_copy(
                velocity_hbm.at[:, pl.ds(x, EDGE), pl.ds(y, EDGE), pl.ds(z, LANES)],
                speeds.at[slot], sems.at[slot, 0],
            ),
            pltpu.make_async_copy(
                frac_hbm.at[pl.ds(x, EDGE), pl.ds(y, EDGE), pl.ds(z, LANES)],
                fracs.at[slot], sems.at[slot, 1],
            ),
        )

    def begin(slot, _):
        for copy in copies(slot):
            copy.start()
        return 0

    lax.fori_loop(0, members * CAP, begin, 0)

    parcels = parcels_ref.shape[-1]

    def sample(slot, member, place):
        for copy in copies(slot):
            copy.wait()
        block = table[slot]
        shift = block % blocks_z * EDGE % LANES
        cell = parcels_ref[member, 5, place:place + 1, :].astype(jnp.int32)
        third = jnp.bitwise_and(cell, EDGE - 1)
        tile = jnp.concatenate(
            [speeds[slot, k].reshape(EDGE * EDGE, LANES) for k in range(3)]
            + [fracs[slot].reshape(EDGE * EDGE, LANES).astype(BF16)],
            axis=1,
        )
        row = lax.broadcasted_iota(jnp.int32, (4 * EDGE, 4 * LANES), 0)
        column = lax.broadcasted_iota(jnp.int32, (4 * EDGE, 4 * LANES), 1)
        wanted = row // EDGE * LANES + row % EDGE + shift
        picker = jnp.where(column == wanted, 1.0, 0.0).astype(BF16)
        window = lax.dot_general(
            picker, tile, (((1,), (1,)), ((), ())), preferred_element_type=F32
        ).astype(BF16)
        spread = jnp.dot(window, rows_of_cell(cell), preferred_element_type=F32)
        lane = lax.broadcasted_iota(jnp.int32, (EDGE, parcels), 0)
        mask = lane == third
        picked = [
            jnp.sum(
                jnp.where(mask, spread[k * EDGE:(k + 1) * EDGE], 0.0), axis=0, keepdims=True
            )
            for k in range(4)
        ]
        filled = block >= 0
        return [jnp.where(filled, value, 0.0) for value in picked[:3]] + [
            jnp.where(filled, picked[3], 1.0)
        ]

    def one_member(member, _):
        first = sample(member * CAP, member, 0)
        second = sample(member * CAP + 1, member, 1)
        rows = [value for pair in zip(first, second) for value in pair]
        out_ref[member] = jnp.concatenate(rows, axis=0).astype(BF16)
        return 0

    lax.fori_loop(0, members, one_member, 0)


def sample_blocks(block_ids, owners, parcels, volume_frac, velocity):
    nx, ny, nz = volume_frac.shape
    members, _, _, count = parcels.shape
    slots = members * CAP
    return pl.pallas_call(
        functools.partial(sample_body, ny // EDGE, nz // EDGE),
        in_specs=[
            pl.BlockSpec(memory_space=pltpu.SMEM),
            pl.BlockSpec(memory_space=pltpu.SMEM),
            pl.BlockSpec(memory_space=pltpu.VMEM),
            pl.BlockSpec(memory_space=pl.ANY),
            pl.BlockSpec(memory_space=pl.ANY),
        ],
        out_specs=pl.BlockSpec(memory_space=pltpu.VMEM),
        out_shape=jax.ShapeDtypeStruct((members, 4 * CAP, count), BF16),
        scratch_shapes=[
            pltpu.VMEM((slots, 3, EDGE, EDGE, LANES), BF16),
            pltpu.VMEM((slots, EDGE, EDGE, LANES), F32),
            pltpu.SMEM((slots,), jnp.int32),
            pltpu.SMEM((members,), jnp.int32),
            pltpu.SemaphoreType.DMA((slots, 2)),
        ],
        compiler_params=params(),
        name="sample",
    )(block_ids, owners, parcels, volume_frac, velocity)


def advance_body(
    blocks_y, blocks_z,
    block_sm, owner_sm, parcels_ref, sampled_ref,
    frac_ref, frac_below, frac_above, speed_below, halo_below_x, halo_above_x,
    halo_below_y, halo_above_y, vel_ref,
    frac_out, vel_out,
    table, count, sides,
):
    step = pl.program_id(0)
    steps = pl.num_programs(0)
    members = parcels_ref.shape[0]
    drops = block_sm.shape[0]
    depth, ny, nz = frac_ref.shape

    @pl.when(step == 0)
    def _():
        slot_table(block_sm, owner_sm, table, count, drops, members)

    vel_out[...] = vel_ref[...]
    sides[0:2] = halo_below_y[...].astype(F32)
    sides[2:3] = halo_above_y[...].astype(F32)

    row8 = lax.broadcasted_iota(jnp.int32, (8, nz), 0)
    lane = lax.broadcasted_iota(jnp.int32, (ny, nz), 1)

    def flux(speed, lower, upper):
        return speed * jnp.where(speed > 0.0, lower, upper)

    first = step == 0
    last = step == steps - 1
    f_below = jnp.where(first, halo_below_x[0].astype(F32), frac_below[0])
    u_below = jnp.where(first, halo_below_x[1], speed_below[0, 0]).astype(F32)
    f_above = jnp.where(last, halo_above_x[0].astype(F32), frac_above[0])

    def layer(x, flux_low):
        f = frac_ref[x]
        u = vel_ref[0, x].astype(F32)
        v = vel_ref[1, x].astype(F32)
        w = vel_ref[2, x].astype(F32)
        f_up = jnp.where(x == depth - 1, f_above, frac_ref[jnp.minimum(x + 1, depth - 1)])
        flux_x = flux(u, f, f_up)
        up = pltpu.roll(f, ny - 1, 0)
        top = jnp.where(row8 == 7, sides[2, pl.ds(x, 1), :], up[ny - 8:])
        up = jnp.concatenate([up[:ny - 8], top], axis=0)
        flux_y = flux(v, f, up)
        edge = flux(sides[1, pl.ds(x, 1), :], sides[0, pl.ds(x, 1), :], f[0:1])
        down = pltpu.roll(flux_y, 1, 0)
        low = jnp.where(row8 == 0, edge, down[:8])
        down = jnp.concatenate([low, down[8:]], axis=0)
        right = jnp.where(lane == nz - 1, 0.0, pltpu.roll(f, nz - 1, 1))
        flux_z = flux(w, f, right)
        left = jnp.where(lane == 0, 0.0, pltpu.roll(flux_z, 1, 1))
        change = (flux_x - flux_low) + (flux_y - down) + (flux_z - left)
        frac_out[x] = jnp.minimum(f - courant * change, 1.0)
        return flux_x

    lax.fori_loop(0, depth, layer, flux(u_below, f_below, frac_ref[0]))

    parcels = parcels_ref.shape[-1]

    def place(slot, _):
        block = table[slot]

        @pl.when((block >= 0) & (block // (blocks_y * blocks_z) == step))
        def _():
            member = slot // CAP
            odd = slot % CAP == 1
            by = block // blocks_z % blocks_y
            bz = block % blocks_z
            y = pl.multiple_of(by * EDGE, EDGE)
            z = pl.multiple_of(bz * EDGE // LANES * LANES, LANES)
            shift = bz * EDGE % LANES

            def field(k):
                both = parcels_ref[member, k]
                return jnp.where(odd, both[1:2], both[0:1])

            got = sampled_ref[member].astype(F32)

            def value(k):
                return jnp.where(odd, got[2 * k + 1:2 * k + 2], got[2 * k:2 * k + 1])

            cell = field(5).astype(jnp.int32)
            factor = field(3) * (1.0 - value(3))
            weight = field(4)
            hits = lax.broadcasted_iota(jnp.int32, (LANES, parcels), 0) == (
                jnp.bitwise_and(cell, EDGE - 1) + shift
            )
            deposits = jnp.concatenate(
                [
                    jnp.where(hits, weight * (factor * (value(k) - field(k))), 0.0).astype(BF16)
                    for k in range(3)
                ],
                axis=0,
            )
            source = lax.dot_general(
                rows_of_cell(cell), deposits, (((1,), (1,)), ((), ())),
                preferred_element_type=F32,
            )
            for k in range(3):
                spot = (k, slice(None), pl.ds(y, EDGE), pl.ds(z, LANES))
                added = source[:, k * LANES:(k + 1) * LANES].astype(BF16).astype(F32)
                old = vel_out[spot].astype(F32).reshape(EDGE * EDGE, LANES)
                vel_out[spot] = (old + added).astype(BF16).reshape(EDGE, EDGE, LANES)

        return 0

    lax.fori_loop(0, members * CAP, place, 0)


def advance(block_ids, owners, parcels, sampled, volume_frac, velocity, below_x, above_x, below_y, above_y):
    nx, ny, nz = volume_frac.shape
    members = parcels.shape[0]
    depth = EDGE
    steps = nx // depth
    return pl.pallas_call(
        functools.partial(advance_body, ny // EDGE, nz // EDGE),
        grid=(steps,),
        in_specs=[
            pl.BlockSpec(memory_space=pltpu.SMEM),
            pl.BlockSpec(memory_space=pltpu.SMEM),
            whole(parcels.shape),
            whole(sampled.shape),
            pl.BlockSpec((depth, ny, nz), lambda i: (i, 0, 0)),
            pl.BlockSpec((1, ny, nz), lambda i: (jnp.maximum(i * depth - 1, 0), 0, 0)),
            pl.BlockSpec((1, ny, nz), lambda i: (jnp.minimum((i + 1) * depth, nx - 1), 0, 0)),
            pl.BlockSpec((1, 1, ny, nz), lambda i: (0, jnp.maximum(i * depth - 1, 0), 0, 0)),
            whole(below_x.shape),
            whole(above_x.shape),
            pl.BlockSpec((2, depth, nz), lambda i: (0, i, 0)),
            pl.BlockSpec((1, depth, nz), lambda i: (0, i, 0)),
            pl.BlockSpec((3, depth, ny, nz), lambda i: (0, i, 0, 0)),
        ],
        out_specs=[
            pl.BlockSpec((depth, ny, nz), lambda i: (i, 0, 0)),
            pl.BlockSpec((3, depth, ny, nz), lambda i: (0, i, 0, 0)),
        ],
        out_shape=[
            jax.ShapeDtypeStruct(volume_frac.shape, F32),
            jax.ShapeDtypeStruct(velocity.shape, BF16),
        ],
        scratch_shapes=[
            pltpu.SMEM((members * CAP,), jnp.int32),
            pltpu.SMEM((members,), jnp.int32),
            pltpu.VMEM((3, depth, nz), F32),
        ],
        compiler_params=params(),
        name="advance",
    )(
        block_ids, owners, parcels, sampled,
        volume_frac, volume_frac, volume_frac, velocity, below_x, above_x, below_y, above_y,
        velocity,
    )


def drag_body(vel_ref, rate_ref, sampled_ref, out_ref):
    members = vel_ref.shape[0]
    for member in range(members):
        got = sampled_ref[member].astype(F32)
        factor = rate_ref[member] * (1.0 - got[3 * CAP:4 * CAP])
        for k in range(3):
            old = vel_ref[member, k]
            out_ref[member, k] = old + factor * (got[k * CAP:(k + 1) * CAP] - old)


def drag(vel, rate, sampled):
    return pl.pallas_call(
        drag_body,
        out_shape=jax.ShapeDtypeStruct(vel.shape, F32),
        compiler_params=params(),
        name="drag",
    )(vel, rate, sampled)


def per_device(
    volume_frac,
    velocity,
    drop_block,
    drop_owner,
    parcel_vel,
    parcel_rate,
    parcel_weight,
    parcel_cell,
):
    block_ids = drop_block.reshape(-1)
    owners = drop_owner.reshape(-1)
    vel = jnp.swapaxes(parcel_vel[0, 0], 1, 2)
    rate = parcel_rate[0, 0]
    parcels, up_x, down_x, up_y, down_y = pack(
        volume_frac, velocity, vel, rate, parcel_weight[0, 0], parcel_cell[0, 0]
    )
    parcels_in = lax.all_to_all(parcels, "member", split_axis=0, concat_axis=0, tiled=True)
    below_x = passed_along(up_x, "group", 1)
    above_x = passed_along(down_x, "group", -1)
    below_y = passed_along(up_y, "member", 1)
    above_y = passed_along(down_y, "member", -1)
    sampled = sample_blocks(block_ids, owners, parcels_in, volume_frac, velocity)
    returned = lax.all_to_all(sampled, "member", split_axis=0, concat_axis=0, tiled=True)
    frac_next, velocity_next = advance(
        block_ids, owners, parcels_in, sampled, volume_frac, velocity,
        below_x, above_x, below_y, above_y,
    )
    vel_next = drag(vel, rate, returned)
    parcel_next = jnp.swapaxes(vel_next, 1, 2)[None, None]
    return (frac_next, velocity_next, parcel_next)


def solution(mesh):
    in_specs = (
        P("group", "member", None),
        P(None, "group", "member", None),
        P("group", "member", None),
        P("group", "member", None, None),
        P("group", "member", None, None, None, None),
        P("group", "member", None, None, None),
        P("group", "member", None, None, None),
        P("group", "member", None, None, None),
    )
    out_specs = (
        P("group", "member", None),
        P(None, "group", "member", None),
        P("group", "member", None, None, None, None),
    )
    return jax.shard_map(
        per_device, mesh=mesh, in_specs=in_specs, out_specs=out_specs, check_vma=False
    )
```

time: 480 us -> 72.9 us (0.15); the launches traced: 472 us -> 72.4 us
  local copies, waits for them, and re-layouts: 297 us -> 1.89 us
  matrix products: 86.3 us -> 0 us
  other arithmetic: 57 us -> 0 us
  Pallas kernels: 0 us -> 36.7 us
  starting transfers between devices: 30 us -> 15.3 us
  blocking collectives: 0 us -> 13.6 us
    gather x96 -> x0, local copies, waits for them, and re-layouts: 128 us -> none
    dot_general x11 -> x0, matrix products: 86.3 us -> none  [the longest x1 35.3 us: per_device(): jnp.einsum('sb,skc->bkc', placement, returned, preferred_element_type=jnp...]
    reshape x6 -> x0, local copies, waits for them, and re-layouts: 75.1 us -> none  [the longest x1 68 us: per_device(): block_field.transpose(3, 0, 4, 1, 5, 2, 6)]
    transpose x1 -> x0, local copies, waits for them, and re-layouts: 64.8 us -> none  [per_device(): block_field.transpose(3, 0, 4, 1, 5, 2, 6)]
    pallas_call x0 -> x4, Pallas kernels: none -> 36.7 us  [the longest x1 22.6 us: advance(): pl.pallas_call(functools.partial(advance_body, ny // EDGE, nz // EDGE), g...]
    convert_element_type x10 -> x0, other arithmetic: 22.1 us -> none  [the longest x1 11.8 us: per_device(): (velocity.astype(jnp.float32) + drag_field).astype(jnp.bfloat16)]
    unnamed x23 -> x18, local copies, waits for them, and re-layouts: 17.9 us -> 1.89 us
    mul x7 -> x0, other arithmetic: 15.5 us -> none  [the longest x3 15.2 us: upwind_div(): courant * (jnp.maximum(speed_low, 0.0) * lower_frac + jnp.minimum(speed_l...]
  transfers between devices with their start and end apart: 7 -> 5, of which waited for: 0 -> 1; matrix products, arithmetic and copies ran while one was open for 43% -> 0% of each run, Pallas kernels for 0% -> 31%
where the time goes in v1:
time: 72.9 us; the launch traced here: 72.4 us
  Pallas kernels  36.7 us (50%)
  starting transfers between devices  15.3 us (21%)
  blocking collectives  13.6 us (19%)
  waiting for transfers between devices  4.23 us (6%)
  local copies, waits for them, and re-layouts  1.89 us (3%)
  between operations  0.77 us (1%)
    pallas_call x1, Pallas kernels, advance(): pl.pallas_call(functools.partial(advance_body, ny // EDGE, nz // EDGE), g...  22.6 us
    all_to_all x1, blocking collectives, per_device(): lax.all_to_all(parcels, 'member', split_axis=0, concat_axis=0, tiled=True)  13.6 us
    ppermute x4, starting transfers between devices, passed_along(): return lax.ppermute(block, axis, route)  11.1 us
    pallas_call x1, Pallas kernels, sample_blocks(): pl.pallas_call(functools.partial(sample_body, ny // EDGE, nz // EDGE), in...  10.1 us
    ppermute x4, waiting for transfers between devices, passed_along(): return lax.ppermute(block, axis, route)  4.22 us
    all_to_all x1, starting transfers between devices, per_device(): lax.all_to_all(sampled, 'member', split_axis=0, concat_axis=0, tiled=True)  4.21 us
    pallas_call x1, Pallas kernels, pack(): pl.pallas_call(pack_body, grid=(1,), in_specs=[whole(vel.shape), whole(ra...  2.4 us
    unnamed x18, local copies, waits for them, and re-layouts  1.89 us
  transfers between devices with their start and end apart: 5, of which 1 were waited for; matrix products, arithmetic and copies ran while one was open for 0% of the time, Pallas kernels for 31%

profile of v1, /device:TPU:6, one launch (start us, length us, event | category | flops | bytes accessed | tf_op | source)
XLA Modules:
  0.0 72.4 jit_solution(6891567526077335593)
XLA Ops:
  0.6 2.4 %pack.1 = (f32[8,6,2,512]{3,2,1,0:T(2,128)}, bf16[2,64,256]{2,1,0:T(8,128)(2,1)}, bf16[1,64,256]{2,1,0:T(8,128)(2,1)}, bf16[2,64,256]{2,1,0:T(8,128)(2,1)}, bf16[1,64,256]{2,1,0:T(8,128)(2,1)}) custom-call(f32[8,3,2,512]{3,2,1,0:T(2,128)} %bitcast.11, f32[8,2,512]{2,1,0:T(2,128)} %bitcast.13, f32[8,2,512]{2,1,0:T(2,128)} %bitcast.16, s32[8,2,512]{2,1,0:T(2,128)} %bitcast.17, ...), custom_call_target="tpu_custom_call" | custom-call | tf_op jit(solution)/shard_map/pack/pallas_call | solution.py:55
  3.0 0.0 copy-start.8
  3.0 0.0 copy-start.7
  3.1 13.6 %all_to_all.10.parcels_ref = f32[8,6,2,512]{3,2,1,0:T(2,128)} all-to-all(f32[8,6,2,512]{3,2,1,0:T(2,128)} %get-tuple-element.10), channel_id=1, replica_groups=mesh['group'=4,'member'=8] {'member'}, dimensions={0} | all-to-all | bytes 393216 | tf_op jit(solution)/shard_map/all_to_all | solution.py:417
  16.6 10.1 %sample.1.sampled_ref = bf16[8,8,512]{2,1,0:T(8,128)(2,1)} custom-call(s32[16]{0:T(128)} %bitcast.18, s32[16]{0:T(128)} %bitcast.20, f32[8,6,2,512]{3,2,1,0:T(2,128)} %all_to_all.10.parcels_ref, f32[64,64,256]{2,1,0:T(8,128)} %frac_above.1, bf16[3,64,64,256]{3,2,1,0:T(8,128)(2,1)} %vel_ref.1), custom_call_target="tpu_custom_call" | custom-call | tf_op jit(solution)/shard_map/sample/pallas_call | solution.py:203
  26.7 4.2 %all-to-all-start.1 = ((bf16[8,8,512]{2,1,0:T(8,128)(2,1)}), bf16[8,8,512]{2,1,0:T(8,128)(2,1)S(1)}, u32[]{:S(2)}, u32[]{:S(2)}) async-start(bf16[8,8,512]{2,1,0:T(8,128)(2,1)} %sample.1.sampled_ref), calls=%async_computation.1 | async-start | bytes 131072 | tf_op jit(solution)/shard_map/all_to_all | solution.py:423
  30.9 0.0 copy-done.6
  30.9 1.9 %collective-permute-start = (bf16[2,64,256]{2,1,0:T(8,128)(2,1)S(1)}, bf16[2,64,256]{2,1,0:T(8,128)(2,1)S(1)}, u32[]{:S(2)}, u32[]{:S(2)}) collective-permute-start(bf16[2,64,256]{2,1,0:T(8,128)(2,1)S(1)} %copy-done.6), channel_id=1, source_target_pairs={{0,8},{8,16},{16,24},{1,9},{9,17},{17,25},{2,10},{10,18},{18,26},{... | collective-permute-start | bytes 196616 | tf_op jit(solution)/shard_map/ppermute | solution.py:24
  32.8 0.0 copy-done.5
  32.9 3.4 %collective-permute-start.2 = (bf16[2,64,256]{2,1,0:T(8,128)(2,1)S(1)}, bf16[2,64,256]{2,1,0:T(8,128)(2,1)S(1)}, u32[]{:S(2)}, u32[]{:S(2)}) collective-permute-start(bf16[2,64,256]{2,1,0:T(8,128)(2,1)S(1)} %copy-done.5), channel_id=1, source_target_pairs={{0,1},{1,2},{2,3},{3,4},{4,5},{5,6},{6,7},{8,9},{9,10},{10,11},{11... | collective-permute-start | bytes 196616 | tf_op jit(solution)/shard_map/ppermute | solution.py:24
  36.3 3.4 %collective-permute-start.1 = (bf16[1,64,256]{2,1,0:T(8,128)(2,1)S(1)}, bf16[1,64,256]{2,1,0:T(8,128)(2,1)S(1)}, u32[]{:S(2)}, u32[]{:S(2)}) collective-permute-start(bf16[1,64,256]{2,1,0:T(8,128)(2,1)S(1)} %copy-done.8), channel_id=1, source_target_pairs={{8,0},{16,8},{24,16},{9,1},{17,9},{25,17},{10,2},{18,10},{26,18},{... | collective-permute-start | bytes 98312 | tf_op jit(solution)/shard_map/ppermute | solution.py:24
  39.6 2.5 %collective-permute-start.3 = (bf16[1,64,256]{2,1,0:T(8,128)(2,1)S(1)}, bf16[1,64,256]{2,1,0:T(8,128)(2,1)S(1)}, u32[]{:S(2)}, u32[]{:S(2)}) collective-permute-start(bf16[1,64,256]{2,1,0:T(8,128)(2,1)S(1)} %copy-done.7), channel_id=1, source_target_pairs={{1,0},{2,1},{3,2},{4,3},{5,4},{6,5},{7,6},{9,8},{10,9},{11,10},{12... | collective-permute-start | bytes 98312 | tf_op jit(solution)/shard_map/ppermute | solution.py:24
  42.1 0.0 collective-permute-done.1.halo_above_x
  42.1 4.2 %collective-permute-done.3.halo_above_y = bf16[1,64,256]{2,1,0:T(8,128)(2,1)S(1)} collective-permute-done((bf16[1,64,256]{2,1,0:T(8,128)(2,1)S(1)}, bf16[1,64,256]{2,1,0:T(8,128)(2,1)S(1)}, u32[]{:S(2)}, u32[]{:S(2)}) %collective-permute-start.3) | collective-permute-done | bytes 32800 | tf_op jit(solution)/shard_map/ppermute | solution.py:24
  46.3 0.0 collective-permute-done.halo_below_x
  46.3 0.0 collective-permute-done.2.halo_below_y
  46.4 0.6 copy-done.4
  47.0 0.0 copy-done.1
  47.0 0.6 copy-done.2
  47.6 22.6 %advance.1 = (f32[64,64,256]{2,1,0:T(8,128)}, bf16[3,64,64,256]{3,2,1,0:T(8,128)(2,1)}) custom-call(s32[16]{0:T(128)} %bitcast.19, s32[16]{0:T(128)} %bitcast.21, f32[8,6,2,512]{3,2,1,0:T(2,128)} %all_to_all.10.parcels_ref, bf16[8,8,512]{2,1,0:T(8,128)(2,1)} %sample.1.sampled_ref, f32[64,64,256]{2,1,0:T(8,128)} %frac_above.1, f32[64,64,256]{2,1,0:T(8,128)} %frac_above.1, ...), custom_call_target="tpu_custom_call" | custom-call | tf_op jit(solution)/shard_map/advance/pallas_call | solution.py:341
  70.2 0.0 all-to-all-done.1.sampled_ref
  70.2 0.0 copy-start
  70.2 0.6 copy-done
  70.8 1.6 %drag.1 = f32[8,3,2,512]{3,2,1,0:T(2,128)} custom-call(f32[8,3,2,512]{3,2,1,0:T(2,128)} %bitcast.12, f32[8,2,512]{2,1,0:T(2,128)} %bitcast.14, bf16[8,8,512]{2,1,0:T(8,128)(2,1)} %copy-done), custom_call_target="tpu_custom_call" | custom-call | tf_op jit(solution)/shard_map/drag/pallas_call | solution.py:392
  (9 shorter events, 0.0 us)
Async XLA Ops:
  3.0 27.9 %copy-start.6 = (bf16[2,64,256]{2,1,0:T(8,128)(2,1)S(1)}, bf16[2,64,256]{2,1,0:T(8,128)(2,1)}, u32[]{:S(2)}) copy-start(bf16[2,64,256]{2,1,0:T(8,128)(2,1)} %get-tuple-element.11) | copy-start | bytes 196612
  3.0 29.8 %copy-start.5 = (bf16[2,64,256]{2,1,0:T(8,128)(2,1)S(1)}, bf16[2,64,256]{2,1,0:T(8,128)(2,1)}, u32[]{:S(2)}) copy-start(bf16[2,64,256]{2,1,0:T(8,128)(2,1)} %get-tuple-element.13) | copy-start | bytes 196612
  3.0 33.2 %copy-start.8 = (bf16[1,64,256]{2,1,0:T(8,128)(2,1)S(1)}, bf16[1,64,256]{2,1,0:T(8,128)(2,1)}, u32[]{:S(2)}) copy-start(bf16[1,64,256]{2,1,0:T(8,128)(2,1)} %get-tuple-element.12) | copy-start | bytes 98308
  3.0 36.6 %copy-start.7 = (bf16[1,64,256]{2,1,0:T(8,128)(2,1)S(1)}, bf16[1,64,256]{2,1,0:T(8,128)(2,1)}, u32[]{:S(2)}) copy-start(bf16[1,64,256]{2,1,0:T(8,128)(2,1)} %get-tuple-element.14) | copy-start | bytes 98308
  26.7 43.5 %all-to-all-start.1 = ((bf16[8,8,512]{2,1,0:T(8,128)(2,1)}), bf16[8,8,512]{2,1,0:T(8,128)(2,1)S(1)}, u32[]{:S(2)}, u32[]{:S(2)}) async-start(bf16[8,8,512]{2,1,0:T(8,128)(2,1)} %sample.1.sampled_ref), calls=%async_computation.1 | async-start | bytes 131072 | tf_op jit(solution)/shard_map/all_to_all | solution.py:423
  30.9 15.4 %collective-permute-start = (bf16[2,64,256]{2,1,0:T(8,128)(2,1)S(1)}, bf16[2,64,256]{2,1,0:T(8,128)(2,1)S(1)}, u32[]{:S(2)}, u32[]{:S(2)}) collective-permute-start(bf16[2,64,256]{2,1,0:T(8,128)(2,1)S(1)} %copy-done.6), channel_id=1, source_target_pairs={{0,8},{8,16},{16,24},{1,9},{9,17},{17,25},{2,10},{10,18},{18,26},{... | collective-permute-start | bytes 196616 | tf_op jit(solution)/shard_map/ppermute | solution.py:24
  32.9 13.5 %collective-permute-start.2 = (bf16[2,64,256]{2,1,0:T(8,128)(2,1)S(1)}, bf16[2,64,256]{2,1,0:T(8,128)(2,1)S(1)}, u32[]{:S(2)}, u32[]{:S(2)}) collective-permute-start(bf16[2,64,256]{2,1,0:T(8,128)(2,1)S(1)} %copy-done.5), channel_id=1, source_target_pairs={{0,1},{1,2},{2,3},{3,4},{4,5},{5,6},{6,7},{8,9},{9,10},{10,11},{11... | collective-permute-start | bytes 196616 | tf_op jit(solution)/shard_map/ppermute | solution.py:24
  36.3 5.9 %collective-permute-start.1 = (bf16[1,64,256]{2,1,0:T(8,128)(2,1)S(1)}, bf16[1,64,256]{2,1,0:T(8,128)(2,1)S(1)}, u32[]{:S(2)}, u32[]{:S(2)}) collective-permute-start(bf16[1,64,256]{2,1,0:T(8,128)(2,1)S(1)} %copy-done.8), channel_id=1, source_target_pairs={{8,0},{16,8},{24,16},{9,1},{17,9},{25,17},{10,2},{18,10},{26,18},{... | collective-permute-start | bytes 98312 | tf_op jit(solution)/shard_map/ppermute | solution.py:24
  39.6 6.7 %collective-permute-start.3 = (bf16[1,64,256]{2,1,0:T(8,128)(2,1)S(1)}, bf16[1,64,256]{2,1,0:T(8,128)(2,1)S(1)}, u32[]{:S(2)}, u32[]{:S(2)}) collective-permute-start(bf16[1,64,256]{2,1,0:T(8,128)(2,1)S(1)} %copy-done.7), channel_id=1, source_target_pairs={{1,0},{2,1},{3,2},{4,3},{5,4},{6,5},{7,6},{9,8},{10,9},{11,10},{12... | collective-permute-start | bytes 98312 | tf_op jit(solution)/shard_map/ppermute | solution.py:24
  42.1 4.2 %copy-start.3 = (bf16[1,64,256]{2,1,0:T(8,128)(2,1)}, bf16[1,64,256]{2,1,0:T(8,128)(2,1)S(1)}, u32[]{:S(2)}) copy-start(bf16[1,64,256]{2,1,0:T(8,128)(2,1)S(1)} %collective-permute-done.1.halo_above_x) | copy-start | bytes 98308
  46.3 0.6 copy-start.4
  46.3 0.6 copy-start.1
  47.0 0.6 copy-start.2
  70.2 0.6 copy-start

commit v2 on v1

v2 whole, which is shorter than its diff:
```python
import functools

import jax
import jax.numpy as jnp
from jax import lax
from jax.experimental import pallas as pl
from jax.experimental.pallas import tpu as pltpu
from jax.sharding import PartitionSpec as P

CAP = 2
EDGE = 16
LANES = 128
FIELDS = 6
GROUP = 2

courant = 0.025

F32 = jnp.float32
BF16 = jnp.bfloat16


def passed_around(block, axis, distance):
    size = lax.axis_size(axis)
    return lax.ppermute(block, axis, [(i, (i + distance) % size) for i in range(size)])


def whole(shape):
    return pl.BlockSpec(shape, lambda *_: (0,) * len(shape))


def params(**more):
    return pltpu.CompilerParams(vmem_limit_bytes=24 * 1024 * 1024, **more)


def pack_body(
    vel_ref, rate_ref, weight_ref, cell_ref,
    f_first_x, f_last_x, u_last_x, f_first_y, f_last_y, u_last_y,
    parcels_ref, up_x, down_x, up_y, down_y,
):
    parcels_ref[:, 0:3] = vel_ref[...]
    parcels_ref[:, 3] = rate_ref[...]
    parcels_ref[:, 4] = weight_ref[...]
    parcels_ref[:, 5] = cell_ref[...].astype(F32)
    up_x[0] = f_last_x[0].astype(BF16)
    up_x[1] = u_last_x[0, 0]
    down_x[0] = f_first_x[0].astype(BF16)
    up_y[0] = f_last_y[:, 7, :].astype(BF16)
    up_y[1] = u_last_y[0].astype(F32)[:, 15, :].astype(BF16)
    down_y[0] = f_first_y[:, 0, :].astype(BF16)


def pack(volume_frac, velocity, vel, rate, weight, cell):
    nx, ny, nz = volume_frac.shape
    members, _, parcels = rate.shape
    return pl.pallas_call(
        pack_body,
        grid=(1,),
        in_specs=[
            whole(vel.shape),
            whole(rate.shape),
            whole(weight.shape),
            whole(cell.shape),
            pl.BlockSpec((1, ny, nz), lambda i: (0, 0, 0)),
            pl.BlockSpec((1, ny, nz), lambda i: (nx - 1, 0, 0)),
            pl.BlockSpec((1, 1, ny, nz), lambda i: (0, nx - 1, 0, 0)),
            pl.BlockSpec((nx, 8, nz), lambda i: (0, 0, 0)),
            pl.BlockSpec((nx, 8, nz), lambda i: (0, ny // 8 - 1, 0)),
            pl.BlockSpec((1, nx, 16, nz), lambda i: (1, 0, ny // 16 - 1, 0)),
        ],
        out_specs=[
            whole((members, FIELDS, CAP, parcels)),
            whole((2, ny, nz)),
            whole((1, ny, nz)),
            whole((2, nx, nz)),
            whole((1, nx, nz)),
        ],
        out_shape=[
            jax.ShapeDtypeStruct((members, FIELDS, CAP, parcels), F32),
            jax.ShapeDtypeStruct((2, ny, nz), BF16),
            jax.ShapeDtypeStruct((1, ny, nz), BF16),
            jax.ShapeDtypeStruct((2, nx, nz), BF16),
            jax.ShapeDtypeStruct((1, nx, nz), BF16),
        ],
        compiler_params=params(),
        name="pack",
    )(
        *in_hbm(vel, rate, weight, cell),
        *in_hbm(volume_frac, volume_frac, velocity, volume_frac, volume_frac, velocity),
    )


def slot_table(block_sm, owner_sm, table, count, drops, members):
    def clear_count(i, _):
        count[i] = 0
        return 0

    def clear_table(i, _):
        table[i] = -1
        return 0

    lax.fori_loop(0, members, clear_count, 0)
    lax.fori_loop(0, members * CAP, clear_table, 0)

    def enter(j, _):
        owner = owner_sm[j]
        place = count[owner]
        count[owner] = place + 1
        table[owner * CAP + place] = block_sm[j]
        return 0

    lax.fori_loop(0, drops, enter, 0)


def corner(block, blocks_y, blocks_z):
    x = block // (blocks_y * blocks_z) * EDGE
    y = pl.multiple_of(block // blocks_z % blocks_y * EDGE, EDGE)
    z = block % blocks_z * EDGE
    return x, y, pl.multiple_of(z // LANES * LANES, LANES), z % LANES


def rows_of_cell(cell):
    high = lax.shift_right_logical(cell, 4)
    rows = lax.broadcasted_iota(jnp.int32, (EDGE * EDGE, cell.shape[-1]), 0)
    return jnp.where(rows == high, 1.0, 0.0).astype(BF16)


def window_of(shift, velocity_ref, frac_ref, spot):
    tile = jnp.concatenate(
        [velocity_ref[(k,) + spot].reshape(EDGE * EDGE, LANES) for k in range(3)]
        + [frac_ref[spot].reshape(EDGE * EDGE, LANES).astype(BF16)],
        axis=1,
    )
    row = lax.broadcasted_iota(jnp.int32, (4 * EDGE, 4 * LANES), 0)
    column = lax.broadcasted_iota(jnp.int32, (4 * EDGE, 4 * LANES), 1)
    wanted = row // EDGE * LANES + row % EDGE + shift
    picker = jnp.where(column == wanted, 1.0, 0.0).astype(BF16)
    return lax.dot_general(
        picker, tile, (((1,), (1,)), ((), ())), preferred_element_type=F32
    ).astype(BF16)


def advect_body(
    blocks_y, blocks_z,
    block_sm, owner_sm, edge_sm,
    halo_below_x, halo_above_x, halo_below_y, halo_above_y, frac_hbm, vel_hbm,
    frac_next, windows_ref,
    table, count, frac_ref, vel_ref, frac_out, sides, flux_low,
    right_even, right_odd, third_even, third_odd, rest_even, rest_odd, sems,
):
    members = count.shape[0]
    drops = block_sm.shape[0]
    nx, ny, nz = frac_out.shape
    steps = sems.shape[1]
    depth = nx // steps
    chunk = right_even.shape[0]

    def part(step):
        return pl.ds(step * depth, depth)

    def frac_in(step):
        return pltpu.make_async_copy(
            frac_hbm.at[part(step)], frac_ref.at[part(step)], sems.at[0, step]
        )

    def vel_in(step):
        return pltpu.make_async_copy(
            vel_hbm.at[:, part(step)], vel_ref.at[:, part(step)], sems.at[1, step]
        )

    def frac_copy(step):
        return pltpu.make_async_copy(
            frac_out.at[part(step)], frac_next.at[part(step)], sems.at[2, step]
        )

    frac_in(0).start()
    for step in range(steps):
        vel_in(step).start()
        if step + 1 < steps:
            frac_in(step + 1).start()

    slot_table(block_sm, owner_sm, table, count, drops, members)

    inner = [edge_sm[i].astype(F32) for i in range(4)]
    frac_ref[nx] = halo_above_x[0].astype(F32) * inner[1]
    sides[0:2] = halo_below_y[...].astype(F32) * inner[2]
    sides[2:3] = halo_above_y[...].astype(F32) * inner[3]
    row = lax.broadcasted_iota(jnp.int32, (8, LANES), 0)
    row_last, row_first = row == 7, row == 0
    along = lax.broadcasted_iota(jnp.int32, (nz, nz), 0)
    across = lax.broadcasted_iota(jnp.int32, (nz, nz), 1)
    shift_left = jnp.where(along == across + 1, 1.0, 0.0).astype(BF16)
    difference = jnp.where(
        along == across, 1.0, jnp.where(along + 1 == across, -1.0, 0.0)
    ).astype(BF16)

    def flux(speed, lower, upper):
        return speed * jnp.where(speed > 0, lower, upper)

    frac_in(0).wait()
    flux_low[...] = flux(
        halo_below_x[1].astype(F32) * inner[0], halo_below_x[0].astype(F32), frac_ref[0]
    )

    def look_right(piece, right):
        cells = frac_ref[pl.ds(piece * chunk, chunk)].reshape(chunk * ny, nz).astype(BF16)
        right[...] = jnp.dot(cells, shift_left, preferred_element_type=F32).reshape(
            chunk, ny, nz
        )

    def finish(piece, third, rest):
        change = jnp.dot(
            third[...].reshape(chunk * ny, nz), difference, preferred_element_type=F32
        ).reshape(chunk, ny, nz)
        frac_out[pl.ds(piece * chunk, chunk)] = jnp.minimum(rest[...] - courant * change, 1.0)

    def layer(x, level, right, third, rest):
        side = sides[:, pl.ds(x, 1), :]
        for h in range(nz // LANES):
            lanes = slice(LANES * h, LANES * h + LANES)
            here = frac_ref[x, 0:8, lanes]
            edge = flux(side[1, :, lanes], side[0, :, lanes], here[0:1])
            carried = jnp.broadcast_to(edge, (8, LANES))
            turned_f = pltpu.roll(here, 7, 0)
            for p in range(ny // 16):
                pair = slice(16 * p, 16 * p + 16)
                u = vel_ref[0, x, pair, lanes].astype(F32)
                v = vel_ref[1, x, pair, lanes].astype(F32)
                w = vel_ref[2, x, pair, lanes]
                both = frac_ref[x, pair, lanes]
                third[level, pair, lanes] = flux(
                    w, both.astype(BF16), right[level, pair, lanes].astype(BF16)
                )
                for t in (2 * p, 2 * p + 1):
                    rows = slice(8 * t, 8 * t + 8)
                    half = slice(8 * (t % 2), 8 * (t % 2) + 8)
                    here = both[half]
                    out_x = flux(u[half], here, frac_ref[x + 1, rows, lanes])
                    change = out_x - flux_low[rows, lanes]
                    flux_low[rows, lanes] = out_x
                    if t + 1 < ny // 8:
                        following = frac_ref[x, 8 * t + 8:8 * t + 16, lanes]
                        turned_next = pltpu.roll(following, 7, 0)
                    else:
                        turned_next = jnp.broadcast_to(side[2, :, lanes], (8, LANES))
                    up = jnp.where(row_last, turned_next, turned_f)
                    turned_f = turned_next
                    out_y = flux(v[half], here, up)
                    rolled = pltpu.roll(out_y, 1, 0)
                    change = change + (out_y - jnp.where(row_first, carried, rolled))
                    carried = rolled
                    rest[level, rows, lanes] = here - courant * change

    pieces = depth // chunk
    total = nx // chunk
    look_right(0, right_even)

    def one_step(step, _):
        vel_in(step).wait()

        @pl.when(step + 1 < steps)
        def _():
            frac_in(step + 1).wait()

        first = step * pieces
        even = (right_even, third_even, rest_even)
        odd = (right_odd, third_odd, rest_odd)
        for k in range(pieces):
            now, other = (even, odd) if k % 2 == 0 else (odd, even)
            look_right(jnp.minimum(first + k + 1, total - 1), other[0])
            finish(jnp.maximum(first + k - 1, 0), other[1], other[2])
            for level in range(chunk):
                layer((first + k) * chunk + level, level, *now)

        @pl.when(step > 0)
        def _():
            frac_copy(step - 1).start()

        return 0

    lax.fori_loop(0, steps, one_step, 0)
    finish(total - 1, third_odd, rest_odd)
    frac_copy(steps - 1).start()

    def some_windows(first, _):
        for more in range(GROUP * CAP):
            slot = first * GROUP * CAP + more
            x, y, z, shift = corner(jnp.maximum(table[slot], 0), blocks_y, blocks_z)
            spot = (pl.ds(x, EDGE), pl.ds(y, EDGE), pl.ds(z, LANES))
            windows_ref[slot] = window_of(shift, vel_ref, frac_ref, spot)
        return 0

    lax.fori_loop(0, members // GROUP, some_windows, 0)

    for step in range(steps):
        frac_copy(step).wait()


def in_hbm(*arrays):
    return [pltpu.with_memory_space_constraint(array, pltpu.HBM) for array in arrays]


def advect(block_ids, owners, edges, volume_frac, velocity, below_x, above_x, below_y, above_y, members):
    nx, ny, nz = volume_frac.shape
    slots = members * CAP
    steps = nx // 8
    chunk = 4
    return pl.pallas_call(
        functools.partial(advect_body, ny // EDGE, nz // EDGE),
        in_specs=[pl.BlockSpec(memory_space=pltpu.SMEM)] * 3
        + [pl.BlockSpec(memory_space=pltpu.VMEM)] * 4
        + [pl.BlockSpec(memory_space=pltpu.HBM)] * 2,
        out_specs=[
            pl.BlockSpec(memory_space=pltpu.HBM),
            pl.BlockSpec(memory_space=pltpu.VMEM),
        ],
        out_shape=[
            jax.ShapeDtypeStruct(volume_frac.shape, F32),
            jax.ShapeDtypeStruct((slots, 4 * EDGE, EDGE * EDGE), BF16),
        ],
        scratch_shapes=[
            pltpu.SMEM((slots,), jnp.int32),
            pltpu.SMEM((members,), jnp.int32),
            pltpu.VMEM((nx + 1, ny, nz), F32),
            pltpu.VMEM(velocity.shape, BF16),
            pltpu.VMEM(volume_frac.shape, F32),
            pltpu.VMEM((3, nx, nz), F32),
            pltpu.VMEM((ny, nz), F32),
            pltpu.VMEM((chunk, ny, nz), F32),
            pltpu.VMEM((chunk, ny, nz), F32),
            pltpu.VMEM((chunk, ny, nz), BF16),
            pltpu.VMEM((chunk, ny, nz), BF16),
            pltpu.VMEM((chunk, ny, nz), F32),
            pltpu.VMEM((chunk, ny, nz), F32),
            pltpu.SemaphoreType.DMA((3, steps)),
        ],
        compiler_params=params(),
        name="advect",
    )(
        block_ids, owners, edges, below_x, above_x, below_y, above_y,
        *in_hbm(volume_frac, velocity),
    )


def sample_body(block_sm, owner_sm, parcels_ref, windows_ref, out_ref, table, count):
    members = parcels_ref.shape[0]
    parcels = parcels_ref.shape[-1]
    slot_table(block_sm, owner_sm, table, count, block_sm.shape[0], members)

    def sample(slot, member, place):
        cell = parcels_ref[member, 5, place:place + 1, :].astype(jnp.int32)
        spread = jnp.dot(windows_ref[slot], rows_of_cell(cell), preferred_element_type=F32)
        mask = lax.broadcasted_iota(jnp.int32, (EDGE, parcels), 0) == jnp.bitwise_and(
            cell, EDGE - 1
        )
        picked = [
            jnp.sum(
                jnp.where(mask, spread[k * EDGE:(k + 1) * EDGE], 0.0), axis=0, keepdims=True
            )
            for k in range(4)
        ]
        filled = table[slot] >= 0
        return [jnp.where(filled, value, 0.0) for value in picked[:3]] + [
            jnp.where(filled, picked[3], 1.0)
        ]

    def some_members(first_member, _):
        for more in range(GROUP):
            member = first_member * GROUP + more
            first = sample(member * CAP, member, 0)
            second = sample(member * CAP + 1, member, 1)
            rows = [value for pair in zip(first, second) for value in pair]
            out_ref[member] = jnp.concatenate(rows, axis=0).astype(BF16)
        return 0

    lax.fori_loop(0, members // GROUP, some_members, 0)


def sample_parcels(block_ids, owners, parcels, windows):
    members, _, _, count = parcels.shape
    return pl.pallas_call(
        sample_body,
        in_specs=[pl.BlockSpec(memory_space=pltpu.SMEM)] * 2
        + [pl.BlockSpec(memory_space=pltpu.VMEM)] * 2,
        out_specs=pl.BlockSpec(memory_space=pltpu.VMEM),
        out_shape=jax.ShapeDtypeStruct((members, 4 * CAP, count), BF16),
        scratch_shapes=[
            pltpu.SMEM((members * CAP,), jnp.int32),
            pltpu.SMEM((members,), jnp.int32),
        ],
        compiler_params=params(),
        name="sample",
    )(block_ids, owners, parcels, windows)


def source_body(
    blocks_y, blocks_z, block_sm, owner_sm, parcels_ref, sampled_ref, vel_hbm,
    vel_next,
    table, count, vel_out, sources, sems,
):
    members = parcels_ref.shape[0]
    parcels = parcels_ref.shape[-1]
    drops = block_sm.shape[0]
    steps = sems.shape[1]
    depth = EDGE

    def vel_in(step):
        part = pl.ds(step * depth, depth)
        return pltpu.make_async_copy(
            vel_hbm.at[:, part], vel_out.at[:, part], sems.at[0, step]
        )

    def vel_copy(step):
        part = pl.ds(step * depth, depth)
        return pltpu.make_async_copy(
            vel_out.at[:, part], vel_next.at[:, part], sems.at[1, step]
        )

    for step in range(steps):
        vel_in(step).start()
    slot_table(block_sm, owner_sm, table, count, drops, members)

    def source_of(slot, member, place):
        block = table[slot]
        shift = corner(jnp.maximum(block, 0), blocks_y, blocks_z)[3]

        def field(k):
            return parcels_ref[member, k, place:place + 1, :]

        got = sampled_ref[member].astype(F32)

        def value(k):
            return got[2 * k + place:2 * k + place + 1]

        cell = field(5).astype(jnp.int32)
        factor = field(3) * (1.0 - value(3))
        weight = field(4)
        wanted = jnp.where(block >= 0, jnp.bitwise_and(cell, EDGE - 1) + shift, -1)
        hits = lax.broadcasted_iota(jnp.int32, (LANES, parcels), 0) == wanted
        deposits = jnp.concatenate(
            [
                jnp.where(hits, weight * (factor * (value(k) - field(k))), 0.0).astype(BF16)
                for k in range(3)
            ],
            axis=0,
        )
        source = lax.dot_general(
            rows_of_cell(cell), deposits, (((1,), (1,)), ((), ())), preferred_element_type=F32
        )
        sources[slot] = source.astype(BF16)

    def some_members(first_member, _):
        for more in range(GROUP):
            member = first_member * GROUP + more
            for place in range(CAP):
                source_of(member * CAP + place, member, place)
        return 0

    lax.fori_loop(0, members // GROUP, some_members, 0)
    for step in range(steps):
        vel_in(step).wait()

    def add_source(slot, _):
        x, y, z, _ = corner(jnp.maximum(table[slot], 0), blocks_y, blocks_z)
        for k in range(3):
            here = (k, pl.ds(x, EDGE), pl.ds(y, EDGE), pl.ds(z, LANES))
            added = sources[slot, :, k * LANES:(k + 1) * LANES].astype(F32)
            old = vel_out[here].astype(F32).reshape(EDGE * EDGE, LANES)
            vel_out[here] = (old + added).astype(BF16).reshape(EDGE, EDGE, LANES)
        return 0

    lax.fori_loop(0, members * CAP, add_source, 0)
    for step in range(steps):
        vel_copy(step).start()
    for step in range(steps):
        vel_copy(step).wait()


def add_drag(block_ids, owners, parcels, sampled, velocity):
    _, nx, ny, nz = velocity.shape
    members = parcels.shape[0]
    slots = members * CAP
    return pl.pallas_call(
        functools.partial(source_body, ny // EDGE, nz // EDGE),
        in_specs=[pl.BlockSpec(memory_space=pltpu.SMEM)] * 2
        + [pl.BlockSpec(memory_space=pltpu.VMEM)] * 2
        + [pl.BlockSpec(memory_space=pltpu.HBM)],
        out_specs=pl.BlockSpec(memory_space=pltpu.HBM),
        out_shape=jax.ShapeDtypeStruct(velocity.shape, BF16),
        scratch_shapes=[
            pltpu.SMEM((slots,), jnp.int32),
            pltpu.SMEM((members,), jnp.int32),
            pltpu.VMEM(velocity.shape, BF16),
            pltpu.VMEM((slots, EDGE * EDGE, 3 * LANES), BF16),
            pltpu.SemaphoreType.DMA((2, nx // EDGE)),
        ],
        compiler_params=params(),
        name="add_drag",
    )(block_ids, owners, parcels, sampled, *in_hbm(velocity))


def drag_body(vel_ref, rate_ref, sampled_ref, out_ref):
    members = vel_ref.shape[0]
    for member in range(members):
        got = sampled_ref[member].astype(F32)
        factor = rate_ref[member] * (1.0 - got[3 * CAP:4 * CAP])
        for k in range(3):
            old = vel_ref[member, k]
            out_ref[member, k] = old + factor * (got[k * CAP:(k + 1) * CAP] - old)


def drag(vel, rate, sampled):
    return pl.pallas_call(
        drag_body,
        out_shape=jax.ShapeDtypeStruct(vel.shape, F32),
        compiler_params=params(),
        name="drag",
    )(vel, rate, sampled)


def per_device(
    volume_frac,
    velocity,
    drop_block,
    drop_owner,
    parcel_vel,
    parcel_rate,
    parcel_weight,
    parcel_cell,
):
    block_ids = drop_block.reshape(-1)
    owners = drop_owner.reshape(-1)
    vel = jnp.swapaxes(parcel_vel[0, 0], 1, 2)
    rate = parcel_rate[0, 0]
    parcels, up_x, down_x, up_y, down_y = pack(
        volume_frac, velocity, vel, rate, parcel_weight[0, 0], parcel_cell[0, 0]
    )
    below_x = passed_around(up_x, "group", 1)
    above_x = passed_around(down_x, "group", -1)
    below_y = passed_around(up_y, "member", 1)
    above_y = passed_around(down_y, "member", -1)
    parcels_in = lax.all_to_all(parcels, "member", split_axis=0, concat_axis=0, tiled=True)
    edges = jnp.stack(
        [
            lax.axis_index("group") > 0,
            lax.axis_index("group") < lax.axis_size("group") - 1,
            lax.axis_index("member") > 0,
            lax.axis_index("member") < lax.axis_size("member") - 1,
        ]
    ).astype(jnp.int32)
    frac_next, windows = advect(
        block_ids, owners, edges, volume_frac, velocity,
        below_x, above_x, below_y, above_y, rate.shape[0],
    )
    parcels_in, windows = lax.optimization_barrier((parcels_in, windows))
    sampled = sample_parcels(block_ids, owners, parcels_in, windows)
    returned = lax.all_to_all(sampled, "member", split_axis=0, concat_axis=0, tiled=True)
    velocity_next = add_drag(block_ids, owners, parcels_in, sampled, velocity)
    vel_next = drag(vel, rate, returned)
    parcel_next = jnp.swapaxes(vel_next, 1, 2)[None, None]
    return (frac_next, velocity_next, parcel_next)


def solution(mesh):
    in_specs = (
        P("group", "member", None),
        P(None, "group", "member", None),
        P("group", "member", None),
        P("group", "member", None, None),
        P("group", "member", None, None, None, None),
        P("group", "member", None, None, None),
        P("group", "member", None, None, None),
        P("group", "member", None, None, None),
    )
    out_specs = (
        P("group", "member", None),
        P(None, "group", "member", None),
        P("group", "member", None, None, None, None),
    )
    return jax.shard_map(
        per_device, mesh=mesh, in_specs=in_specs, out_specs=out_specs, check_vma=False
    )
```

time: 72.9 us -> 45.1 us (0.62)
  the two profiles are of different devices: /device:TPU:6 before, /device:TPU:0 now
where the time goes in v2:
time: 45.1 us; the launch traced here: 44.7 us
  Pallas kernels  22.4 us (50%)
  starting transfers between devices  18.5 us (41%)
  waiting for transfers between devices  3.08 us (7%)
  between operations  0.72 us (2%)
    pallas_call x1, Pallas kernels, advect(): pl.pallas_call(functools.partial(advect_body, ny // EDGE, nz // EDGE), in...  8.63 us
    pallas_call x1, Pallas kernels, add_drag(): pl.pallas_call(functools.partial(source_body, ny // EDGE, nz // EDGE), in...  8.02 us
    all_to_all x1, starting transfers between devices, per_device(): lax.all_to_all(parcels, 'member', split_axis=0, concat_axis=0, tiled=True)  7.25 us
    ppermute x4, starting transfers between devices, passed_around(): lax.ppermute(block, axis, [(i, (i + distance) % size) for i in range(size)])  6.46 us
    all_to_all x1, starting transfers between devices, per_device(): lax.all_to_all(sampled, 'member', split_axis=0, concat_axis=0, tiled=True)  4.75 us
    ppermute x4, waiting for transfers between devices, passed_around(): lax.ppermute(block, axis, [(i, (i + distance) % size) for i in range(size)])  3.07 us
    pallas_call x1, Pallas kernels, sample_parcels(): pl.pallas_call(sample_body, in_specs=[pl.BlockSpec(memory_space=pltpu.SME...  2.74 us
    pallas_call x1, Pallas kernels, pack(): pl.pallas_call(pack_body, grid=(1,), in_specs=[whole(vel.shape), whole(ra...  2.25 us
  transfers between devices with their start and end apart: 6, of which 2 were waited for; matrix products, arithmetic and copies ran while one was open for 0% of the time, Pallas kernels for 37%

profile of v2, /device:TPU:0, one launch (start us, length us, event | category | flops | bytes accessed | tf_op | source)
XLA Modules:
  0.0 44.7 jit_solution(16262839974540351026)
XLA Ops:
  0.6 0.0 copy-start.2
  0.6 0.0 copy-start.3
  0.7 2.3 %pack.1 = (f32[8,6,2,512]{3,2,1,0:T(2,128)}, bf16[2,64,256]{2,1,0:T(8,128)(2,1)S(1)}, bf16[1,64,256]{2,1,0:T(8,128)(2,1)S(1)}, bf16[2,64,256]{2,1,0:T(8,128)(2,1)S(1)}, bf16[1,64,256]{2,1,0:T(8,128)(2,1)S(1)}) custom-call(f32[8,3,2,512]{3,2,1,0:T(2,128)} %bitcast.15, f32[8,2,512]{2,1,0:T(2,128)} %bitcast.17, f32[8,2,512]{2,1,0:T(2,128)} %bitcast.26, ...), custom_call_target="tpu_custom_call" | custom-call | tf_op jit(solution)/shard_map/pack/pallas_call | solution.py:55
  2.9 7.3 %all-to-all-start = ((f32[8,6,2,512]{3,2,1,0:T(2,128)}), f32[8,6,2,512]{3,2,1,0:T(2,128)S(1)}, u32[]{:S(2)}, u32[]{:S(2)}) async-start(f32[8,6,2,512]{3,2,1,0:T(2,128)} %get-tuple-element.17), calls=%async_computation | async-start | bytes 393216 | tf_op jit(solution)/shard_map/all_to_all | solution.py:541
  10.2 0.0 collective-permute-start
  10.2 1.7 %collective-permute-start.1 = (bf16[1,64,256]{2,1,0:T(8,128)(2,1)S(1)}, bf16[1,64,256]{2,1,0:T(8,128)(2,1)S(1)}, u32[]{:S(2)}, u32[]{:S(2)}) collective-permute-start(bf16[1,64,256]{2,1,0:T(8,128)(2,1)S(1)} %get-tuple-element.13), channel_id=1, source_target_pairs={{0,24},{8,0},{16,8},{24,16},{1,25},{9,1},{17,9},{25,17},{2,26},{10... | collective-permute-start | bytes 98312 | tf_op jit(solution)/shard_map/ppermute | solution.py:24
  11.9 2.0 %collective-permute-start.2 = (bf16[2,64,256]{2,1,0:T(8,128)(2,1)S(1)}, bf16[2,64,256]{2,1,0:T(8,128)(2,1)S(1)}, u32[]{:S(2)}, u32[]{:S(2)}) collective-permute-start(bf16[2,64,256]{2,1,0:T(8,128)(2,1)S(1)} %get-tuple-element.14), channel_id=1, source_target_pairs={{0,1},{1,2},{2,3},{3,4},{4,5},{5,6},{6,7},{7,0},{8,9},{9,10},{10,1... | collective-permute-start | bytes 196616 | tf_op jit(solution)/shard_map/ppermute | solution.py:24
  13.9 2.7 %collective-permute-start.3 = (bf16[1,64,256]{2,1,0:T(8,128)(2,1)S(1)}, bf16[1,64,256]{2,1,0:T(8,128)(2,1)S(1)}, u32[]{:S(2)}, u32[]{:S(2)}) collective-permute-start(bf16[1,64,256]{2,1,0:T(8,128)(2,1)S(1)} %get-tuple-element.15), channel_id=1, source_target_pairs={{0,7},{1,0},{2,1},{3,2},{4,3},{5,4},{6,5},{7,6},{8,15},{9,8},{10,9... | collective-permute-start | bytes 98312 | tf_op jit(solution)/shard_map/ppermute | solution.py:24
  16.6 0.1 add_convert_fusion.edge_sm
  16.7 0.0 collective-permute-done.1.halo_above_x
  16.7 1.5 %collective-permute-done.3.halo_above_y = bf16[1,64,256]{2,1,0:T(8,128)(2,1)S(1)} collective-permute-done((bf16[1,64,256]{2,1,0:T(8,128)(2,1)S(1)}, bf16[1,64,256]{2,1,0:T(8,128)(2,1)S(1)}, u32[]{:S(2)}, u32[]{:S(2)}) %collective-permute-start.3) | collective-permute-done | bytes 32800 | tf_op jit(solution)/shard_map/ppermute | solution.py:24
  18.2 0.0 collective-permute-done.halo_below_x
  18.2 1.5 %collective-permute-done.2.halo_below_y = bf16[2,64,256]{2,1,0:T(8,128)(2,1)S(1)} collective-permute-done((bf16[2,64,256]{2,1,0:T(8,128)(2,1)S(1)}, bf16[2,64,256]{2,1,0:T(8,128)(2,1)S(1)}, u32[]{:S(2)}, u32[]{:S(2)}) %collective-permute-start.2) | collective-permute-done | bytes 65568 | tf_op jit(solution)/shard_map/ppermute | solution.py:24
  19.8 0.0 copy-done.2
  19.8 0.0 copy-done.3
  19.8 8.6 %advect.1 = (f32[64,64,256]{2,1,0:T(8,128)}, bf16[16,64,256]{2,1,0:T(8,128)(2,1)S(1)}) custom-call(s32[16]{0:T(128)S(1)} %bitcast.19, s32[16]{0:T(128)S(1)} %bitcast.22, s32[4]{0:T(128)S(1)} %add_convert_fusion.edge_sm, bf16[2,64,256]{2,1,0:T(8,128)(2,1)S(1)} %collective-permute-done.halo_below_x, ...), custom_call_target="tpu_custom_call" | custom-call | tf_op jit(solution)/shard_map/advect/pallas_call | solution.py:307
  28.4 0.0 all-to-all-done.parcels_ref
  28.4 2.7 %sample.1.sampled_ref = bf16[8,8,512]{2,1,0:T(8,128)(2,1)} custom-call(s32[16]{0:T(128)S(1)} %bitcast.20, s32[16]{0:T(128)S(1)} %bitcast.23, f32[8,6,2,512]{3,2,1,0:T(2,128)S(1)} %all-to-all-done.parcels_ref, bf16[16,64,256]{2,1,0:T(8,128)(2,1)S(1)} %get-tuple-element.20.windows_ref), custom_call_target="tpu_custom_call" | custom-call | tf_op jit(solution)/shard_map/sample/pallas_call | solution.py:380
  31.2 4.8 %all-to-all-start.1 = ((bf16[8,8,512]{2,1,0:T(8,128)(2,1)}), bf16[8,8,512]{2,1,0:T(8,128)(2,1)S(1)}, u32[]{:S(2)}, u32[]{:S(2)}) async-start(bf16[8,8,512]{2,1,0:T(8,128)(2,1)} %sample.1.sampled_ref), calls=%async_computation.1 | async-start | bytes 131072 | tf_op jit(solution)/shard_map/all_to_all | solution.py:556
  35.9 0.0 copy-start.1
  35.9 8.0 %add_drag.1 = bf16[3,64,64,256]{3,2,1,0:T(8,128)(2,1)} custom-call(s32[16]{0:T(128)S(1)} %bitcast.21, s32[16]{0:T(128)S(1)} %bitcast.24, f32[8,6,2,512]{3,2,1,0:T(2,128)S(1)} %all-to-all-done.parcels_ref, bf16[8,8,512]{2,1,0:T(8,128)(2,1)} %sample.1.sampled_ref, bf16[3,64,64,256]{3,2,1,0:T(8,128)(2,1)} %vel_hbm.3), custom_call_target="tpu_custom_call" | custom-call | tf_op jit(solution)/shard_map/add_drag/pallas_call | solution.py:482
  44.0 0.0 all-to-all-done.1.sampled_ref
  44.0 0.0 copy-done
  44.0 0.7 %drag.1 = f32[8,3,2,512]{3,2,1,0:T(2,128)} custom-call(f32[8,3,2,512]{3,2,1,0:T(2,128)S(1)} %bitcast.16, f32[8,2,512]{2,1,0:T(2,128)S(1)} %bitcast.18, bf16[8,8,512]{2,1,0:T(8,128)(2,1)S(1)} %all-to-all-done.1.sampled_ref), custom_call_target="tpu_custom_call" | custom-call | tf_op jit(solution)/shard_map/drag/pallas_call | solution.py:512
  (2 shorter events, 0.0 us)
Async XLA Ops:
  0.6 19.1 %copy-start.2 = (s32[1,1,16]{2,1,0:T(1,128)S(1)}, s32[1,1,16]{2,1,0:T(1,128)}, u32[]{:S(2)}) copy-start(s32[1,1,16]{2,1,0:T(1,128)} %param.10) | copy-start | bytes 196
  0.6 19.1 %copy-start.3 = (s32[1,1,16,1]{2,3,1,0:T(1,128)S(1)}, s32[1,1,16,1]{2,3,1,0:T(1,128)}, u32[]{:S(2)}) copy-start(s32[1,1,16,1]{2,3,1,0:T(1,128)} %param.11) | copy-start | bytes 196
  2.9 25.5 %all-to-all-start = ((f32[8,6,2,512]{3,2,1,0:T(2,128)}), f32[8,6,2,512]{3,2,1,0:T(2,128)S(1)}, u32[]{:S(2)}, u32[]{:S(2)}) async-start(f32[8,6,2,512]{3,2,1,0:T(2,128)} %get-tuple-element.17), calls=%async_computation | async-start | bytes 393216 | tf_op jit(solution)/shard_map/all_to_all | solution.py:541
  10.2 8.1 %collective-permute-start = (bf16[2,64,256]{2,1,0:T(8,128)(2,1)S(1)}, bf16[2,64,256]{2,1,0:T(8,128)(2,1)S(1)}, u32[]{:S(2)}, u32[]{:S(2)}) collective-permute-start(bf16[2,64,256]{2,1,0:T(8,128)(2,1)S(1)} %get-tuple-element.12), channel_id=1, source_target_pairs={{0,8},{8,16},{16,24},{24,0},{1,9},{9,17},{17,25},{25,1},{2,10},{10... | collective-permute-start | bytes 196616 | tf_op jit(solution)/shard_map/ppermute | solution.py:24
  10.2 6.5 %collective-permute-start.1 = (bf16[1,64,256]{2,1,0:T(8,128)(2,1)S(1)}, bf16[1,64,256]{2,1,0:T(8,128)(2,1)S(1)}, u32[]{:S(2)}, u32[]{:S(2)}) collective-permute-start(bf16[1,64,256]{2,1,0:T(8,128)(2,1)S(1)} %get-tuple-element.13), channel_id=1, source_target_pairs={{0,24},{8,0},{16,8},{24,16},{1,25},{9,1},{17,9},{25,17},{2,26},{10... | collective-permute-start | bytes 98312 | tf_op jit(solution)/shard_map/ppermute | solution.py:24
  11.9 7.9 %collective-permute-start.2 = (bf16[2,64,256]{2,1,0:T(8,128)(2,1)S(1)}, bf16[2,64,256]{2,1,0:T(8,128)(2,1)S(1)}, u32[]{:S(2)}, u32[]{:S(2)}) collective-permute-start(bf16[2,64,256]{2,1,0:T(8,128)(2,1)S(1)} %get-tuple-element.14), channel_id=1, source_target_pairs={{0,1},{1,2},{2,3},{3,4},{4,5},{5,6},{6,7},{7,0},{8,9},{9,10},{10,1... | collective-permute-start | bytes 196616 | tf_op jit(solution)/shard_map/ppermute | solution.py:24
  13.9 4.3 %collective-permute-start.3 = (bf16[1,64,256]{2,1,0:T(8,128)(2,1)S(1)}, bf16[1,64,256]{2,1,0:T(8,128)(2,1)S(1)}, u32[]{:S(2)}, u32[]{:S(2)}) collective-permute-start(bf16[1,64,256]{2,1,0:T(8,128)(2,1)S(1)} %get-tuple-element.15), channel_id=1, source_target_pairs={{0,7},{1,0},{2,1},{3,2},{4,3},{5,4},{6,5},{7,6},{8,15},{9,8},{10,9... | collective-permute-start | bytes 98312 | tf_op jit(solution)/shard_map/ppermute | solution.py:24
  31.2 12.8 %all-to-all-start.1 = ((bf16[8,8,512]{2,1,0:T(8,128)(2,1)}), bf16[8,8,512]{2,1,0:T(8,128)(2,1)S(1)}, u32[]{:S(2)}, u32[]{:S(2)}) async-start(bf16[8,8,512]{2,1,0:T(8,128)(2,1)} %sample.1.sampled_ref), calls=%async_computation.1 | async-start | bytes 131072 | tf_op jit(solution)/shard_map/all_to_all | solution.py:556
  35.9 8.1 %copy-start = (f32[1,1,8,2,3,512]{5,3,4,2,1,0:T(2,128)S(1)}, f32[1,1,8,2,3,512]{5,3,4,2,1,0:T(2,128)}, u32[]{:S(2)}) copy-start(f32[1,1,8,2,3,512]{5,3,4,2,1,0:T(2,128)} %param.12) | copy-start | bytes 294916
  35.9 8.1 %copy-start.1 = (f32[1,1,8,2,512]{4,3,2,1,0:T(2,128)S(1)}, f32[1,1,8,2,512]{4,3,2,1,0:T(2,128)}, u32[]{:S(2)}) copy-start(f32[1,1,8,2,512]{4,3,2,1,0:T(2,128)} %param.13) | copy-start | bytes 98308

commit v3 on v2

--- a/solution.py
+++ b/solution.py
@@ -119,9 +119,10 @@
 
 
 def rows_of_cell(cell):
-    high = lax.shift_right_logical(cell, 4)
+    high = lax.shift_right_logical(cell, 4).astype(F32).astype(BF16)
     rows = lax.broadcasted_iota(jnp.int32, (EDGE * EDGE, cell.shape[-1]), 0)
-    return jnp.where(rows == high, 1.0, 0.0).astype(BF16)
+    hits = rows.astype(F32).astype(BF16) == high
+    return jnp.where(hits, jnp.ones_like(high), jnp.zeros_like(high))
 
 
 def window_of(shift, velocity_ref, frac_ref, spot):
@@ -141,11 +142,11 @@
 
 def advect_body(
     blocks_y, blocks_z,
-    block_sm, owner_sm, edge_sm,
+    block_hbm, owner_hbm, edge_sm,
     halo_below_x, halo_above_x, halo_below_y, halo_above_y, frac_hbm, vel_hbm,
     frac_next, windows_ref,
-    table, count, frac_ref, vel_ref, frac_out, sides, flux_low,
-    right_even, right_odd, third_even, third_odd, rest_even, rest_odd, sems,
+    block_sm, owner_sm, table, count, frac_ref, vel_ref, frac_out, sides, flux_low,
+    right_even, right_odd, third_even, third_odd, rest_even, rest_odd, sems, scalar_sems,
 ):
     members = count.shape[0]
     drops = block_sm.shape[0]
@@ -163,21 +164,33 @@
         )
 
     def vel_in(step):
-        return pltpu.make_async_copy(
-            vel_hbm.at[:, part(step)], vel_ref.at[:, part(step)], sems.at[1, step]
-        )
+        return [
+            pltpu.make_async_copy(
+                vel_hbm.at[k, part(step)], vel_ref.at[k, part(step)], sems.at[2 + k, step]
+            )
+            for k in range(3)
+        ]
 
     def frac_copy(step):
         return pltpu.make_async_copy(
-            frac_out.at[part(step)], frac_next.at[part(step)], sems.at[2, step]
+            frac_out.at[part(step)], frac_next.at[part(step)], sems.at[1, step]
         )
 
     frac_in(0).start()
     for step in range(steps):
-        vel_in(step).start()
+        for copy in vel_in(step):
+            copy.start()
         if step + 1 < steps:
             frac_in(step + 1).start()
 
+    scalars = [
+        pltpu.make_async_copy(block_hbm, block_sm, scalar_sems.at[0]),
+        pltpu.make_async_copy(owner_hbm, owner_sm, scalar_sems.at[1]),
+    ]
+    for copy in scalars:
+        copy.start()
+    for copy in scalars:
+        copy.wait()
     slot_table(block_sm, owner_sm, table, count, drops, members)
 
     inner = [edge_sm[i].astype(F32) for i in range(4)]
@@ -255,7 +268,8 @@
     look_right(0, right_even)
 
     def one_step(step, _):
-        vel_in(step).wait()
+        for copy in vel_in(step):
+            copy.wait()
 
         @pl.when(step + 1 < steps)
         def _():
@@ -281,12 +295,17 @@
     finish(total - 1, third_odd, rest_odd)
     frac_copy(steps - 1).start()
 
+    nothing = jnp.where(
+        lax.broadcasted_iota(jnp.int32, (4 * EDGE, EDGE * EDGE), 0) >= 3 * EDGE, 1.0, 0.0
+    ).astype(BF16)
+
     def some_windows(first, _):
         for more in range(GROUP * CAP):
             slot = first * GROUP * CAP + more
             x, y, z, shift = corner(jnp.maximum(table[slot], 0), blocks_y, blocks_z)
             spot = (pl.ds(x, EDGE), pl.ds(y, EDGE), pl.ds(z, LANES))
-            windows_ref[slot] = window_of(shift, vel_ref, frac_ref, spot)
+            window = window_of(shift, vel_ref, frac_ref, spot)
+            windows_ref[slot] = jnp.where(table[slot] >= 0, window, nothing)
         return 0
 
     lax.fori_loop(0, members // GROUP, some_windows, 0)
@@ -306,7 +325,8 @@
     chunk = 4
     return pl.pallas_call(
         functools.partial(advect_body, ny // EDGE, nz // EDGE),
-        in_specs=[pl.BlockSpec(memory_space=pltpu.SMEM)] * 3
+        in_specs=[pl.BlockSpec(memory_space=pltpu.HBM)] * 2
+        + [pl.BlockSpec(memory_space=pltpu.SMEM)]
         + [pl.BlockSpec(memory_space=pltpu.VMEM)] * 4
         + [pl.BlockSpec(memory_space=pltpu.HBM)] * 2,
         out_specs=[
@@ -318,6 +338,8 @@
             jax.ShapeDtypeStruct((slots, 4 * EDGE, EDGE * EDGE), BF16),
         ],
         scratch_shapes=[
+            pltpu.SMEM(block_ids.shape, jnp.int32),
+            pltpu.SMEM(owners.shape, jnp.int32),
             pltpu.SMEM((slots,), jnp.int32),
             pltpu.SMEM((members,), jnp.int32),
             pltpu.VMEM((nx + 1, ny, nz), F32),
@@ -331,20 +353,25 @@
             pltpu.VMEM((chunk, ny, nz), BF16),
             pltpu.VMEM((chunk, ny, nz), F32),
             pltpu.VMEM((chunk, ny, nz), F32),
-            pltpu.SemaphoreType.DMA((3, steps)),
+            pltpu.SemaphoreType.DMA((5, steps)),
+            pltpu.SemaphoreType.DMA((2,)),
         ],
         compiler_params=params(),
+        cost_estimate=pl.CostEstimate(
+            flops=8 * (60 * volume_frac.size + 4 * volume_frac.size * nz),
+            bytes_accessed=8 * (2 * volume_frac.size * 4 + velocity.size * 2),
+            transcendentals=0,
+        ),
         name="advect",
     )(
-        block_ids, owners, edges, below_x, above_x, below_y, above_y,
+        *in_hbm(block_ids, owners), edges, below_x, above_x, below_y, above_y,
         *in_hbm(volume_frac, velocity),
     )
 
 
-def sample_body(block_sm, owner_sm, parcels_ref, windows_ref, out_ref, table, count):
+def sample_body(parcels_ref, windows_ref, out_ref, kept_ref):
     members = parcels_ref.shape[0]
     parcels = parcels_ref.shape[-1]
-    slot_table(block_sm, owner_sm, table, count, block_sm.shape[0], members)
 
     def sample(slot, member, place):
         cell = parcels_ref[member, 5, place:place + 1, :].astype(jnp.int32)
@@ -352,93 +379,124 @@
         mask = lax.broadcasted_iota(jnp.int32, (EDGE, parcels), 0) == jnp.bitwise_and(
             cell, EDGE - 1
         )
-        picked = [
+        return [
             jnp.sum(
                 jnp.where(mask, spread[k * EDGE:(k + 1) * EDGE], 0.0), axis=0, keepdims=True
             )
             for k in range(4)
         ]
-        filled = table[slot] >= 0
-        return [jnp.where(filled, value, 0.0) for value in picked[:3]] + [
-            jnp.where(filled, picked[3], 1.0)
-        ]
+
+    together = 2 * GROUP
 
     def some_members(first_member, _):
-        for more in range(GROUP):
-            member = first_member * GROUP + more
+        for more in range(together):
+            member = first_member * together + more
             first = sample(member * CAP, member, 0)
             second = sample(member * CAP + 1, member, 1)
             rows = [value for pair in zip(first, second) for value in pair]
-            out_ref[member] = jnp.concatenate(rows, axis=0).astype(BF16)
+            sampled = jnp.concatenate(rows, axis=0).astype(BF16)
+            out_ref[member] = sampled
+            kept_ref[member] = sampled
         return 0
 
-    lax.fori_loop(0, members // GROUP, some_members, 0)
-
-
-def sample_parcels(block_ids, owners, parcels, windows):
+    lax.fori_loop(0, members // together, some_members, 0)
+
+
+def sample_parcels(parcels, windows):
     members, _, _, count = parcels.shape
     return pl.pallas_call(
         sample_body,
-        in_specs=[pl.BlockSpec(memory_space=pltpu.SMEM)] * 2
-        + [pl.BlockSpec(memory_space=pltpu.VMEM)] * 2,
-        out_specs=pl.BlockSpec(memory_space=pltpu.VMEM),
-        out_shape=jax.ShapeDtypeStruct((members, 4 * CAP, count), BF16),
-        scratch_shapes=[
-            pltpu.SMEM((members * CAP,), jnp.int32),
-            pltpu.SMEM((members,), jnp.int32),
-        ],
+        in_specs=[pl.BlockSpec(memory_space=pltpu.VMEM)] * 2,
+        out_specs=[pl.BlockSpec(memory_space=pltpu.VMEM)] * 2,
+        out_shape=[jax.ShapeDtypeStruct((members, 4 * CAP, count), BF16)] * 2,
         compiler_params=params(),
         name="sample",
-    )(block_ids, owners, parcels, windows)
+    )(parcels, windows)
 
 
 def source_body(
-    blocks_y, blocks_z, block_sm, owner_sm, parcels_ref, sampled_ref, vel_hbm,
+    blocks_y, blocks_z, block_hbm, owner_hbm, parcels_ref, sampled_ref, vel_hbm,
     vel_next,
-    table, count, vel_out, sources, sems,
+    block_sm, owner_sm, table, count, order, begins, ends, vel_ref, sems, scalar_sems,
 ):
     members = parcels_ref.shape[0]
     parcels = parcels_ref.shape[-1]
-    drops = block_sm.shape[0]
+    slots = members * CAP
     steps = sems.shape[1]
-    depth = EDGE
+    together = GROUP * CAP
+    rounds = slots // together
 
     def vel_in(step):
-        part = pl.ds(step * depth, depth)
-        return pltpu.make_async_copy(
-            vel_hbm.at[:, part], vel_out.at[:, part], sems.at[0, step]
-        )
+        return [
+            pltpu.make_async_copy(
+                vel_hbm.at[k, pl.ds(step * EDGE, EDGE)], vel_ref.at[k, pl.ds(step * EDGE, EDGE)],
+                sems.at[k, step],
+            )
+            for k in range(3)
+        ]
 
     def vel_copy(step):
-        part = pl.ds(step * depth, depth)
-        return pltpu.make_async_copy(
-            vel_out.at[:, part], vel_next.at[:, part], sems.at[1, step]
-        )
-
+        return [
+            pltpu.make_async_copy(
+                vel_ref.at[k, pl.ds(step * EDGE, EDGE)], vel_next.at[k, pl.ds(step * EDGE, EDGE)],
+                sems.at[3 + k, step],
+            )
+            for k in range(3)
+        ]
+
+    scalars = [
+        pltpu.make_async_copy(block_hbm, block_sm, scalar_sems.at[0]),
+        pltpu.make_async_copy(owner_hbm, owner_sm, scalar_sems.at[1]),
+    ]
+    for copy in scalars:
+        copy.start()
     for step in range(steps):
-        vel_in(step).start()
-    slot_table(block_sm, owner_sm, table, count, drops, members)
-
-    def source_of(slot, member, place):
+        for copy in vel_in(step):
+            copy.start()
+    for copy in scalars:
+        copy.wait()
+    slot_table(block_sm, owner_sm, table, count, block_sm.shape[0], members)
+
+    filled = 0
+    for step in range(steps):
+        begins[step] = filled
+
+        def enter(slot, at):
+            mine = jnp.maximum(table[slot], 0) // (blocks_y * blocks_z) == step
+
+            @pl.when(mine)
+            def _():
+                order[at] = slot
+
+            return at + mine.astype(jnp.int32)
+
+        filled = lax.fori_loop(0, slots, enter, filled)
+        ends[step] = filled
+
+    def source_of(slot):
         block = table[slot]
-        shift = corner(jnp.maximum(block, 0), blocks_y, blocks_z)[3]
-
-        def field(k):
-            return parcels_ref[member, k, place:place + 1, :]
-
+        spot = corner(jnp.maximum(block, 0), blocks_y, blocks_z)
+        member = slot // CAP
+        odd = slot % CAP == 1
+        both = [parcels_ref[member, k] for k in range(FIELDS)]
+        field = [jnp.where(odd, value[1:2], value[0:1]) for value in both]
         got = sampled_ref[member].astype(F32)
-
-        def value(k):
-            return got[2 * k + place:2 * k + place + 1]
-
-        cell = field(5).astype(jnp.int32)
-        factor = field(3) * (1.0 - value(3))
-        weight = field(4)
-        wanted = jnp.where(block >= 0, jnp.bitwise_and(cell, EDGE - 1) + shift, -1)
-        hits = lax.broadcasted_iota(jnp.int32, (LANES, parcels), 0) == wanted
+        value = [
+            jnp.where(odd, got[CAP * k + 1:CAP * k + 2], got[CAP * k:CAP * k + 1])
+            for k in range(4)
+        ]
+        cell = field[5].astype(jnp.int32)
+        factor = field[3] * (1.0 - value[3])
+        wanted = jnp.where(block >= 0, jnp.bitwise_and(cell, EDGE - 1), -1)
+        third = lax.broadcasted_iota(jnp.int32, (EDGE, parcels), 0).astype(F32).astype(BF16)
+        hits = third == wanted.astype(F32).astype(BF16)
         deposits = jnp.concatenate(
             [
-                jnp.where(hits, weight * (factor * (value(k) - field(k))), 0.0).astype(BF16)
+                jnp.where(
+                    hits,
+                    (field[4] * (factor * (value[k] - field[k]))).astype(BF16),
+                    jnp.zeros((1, parcels), BF16),
+                )
                 for k in range(3)
             ],
             axis=0,
@@ -446,56 +504,77 @@
         source = lax.dot_general(
             rows_of_cell(cell), deposits, (((1,), (1,)), ((), ())), preferred_element_type=F32
         )
-        sources[slot] = source.astype(BF16)
-
-    def some_members(first_member, _):
-        for more in range(GROUP):
-            member = first_member * GROUP + more
-            for place in range(CAP):
-                source_of(member * CAP + place, member, place)
-        return 0
-
-    lax.fori_loop(0, members // GROUP, some_members, 0)
-    for step in range(steps):
-        vel_in(step).wait()
-
-    def add_source(slot, _):
-        x, y, z, _ = corner(jnp.maximum(table[slot], 0), blocks_y, blocks_z)
+        wide = jnp.concatenate([source, jnp.zeros((EDGE * EDGE, LANES - 3 * EDGE), F32)], axis=1)
+        at = lax.broadcasted_iota(jnp.int32, (EDGE * EDGE, LANES), 1) - spot[3]
+        inside = (at >= 0) & (at < EDGE)
+        placed = [
+            jnp.where(inside, pltpu.roll(wide, lax.rem(spot[3] + LANES - k * EDGE, LANES), 1), 0.0)
+            for k in range(3)
+        ]
+        return spot, [piece.astype(BF16) for piece in placed]
+
+    def add_source(spot, source):
+        x, y, z, _ = spot
         for k in range(3):
             here = (k, pl.ds(x, EDGE), pl.ds(y, EDGE), pl.ds(z, LANES))
-            added = sources[slot, :, k * LANES:(k + 1) * LANES].astype(F32)
-            old = vel_out[here].astype(F32).reshape(EDGE * EDGE, LANES)
-            vel_out[here] = (old + added).astype(BF16).reshape(EDGE, EDGE, LANES)
+            vel_ref[here] = vel_ref[here] + source[k].reshape(EDGE, EDGE, LANES)
+
+    def one_round(turn, _):
+        found = [source_of(order[turn * together + more]) for more in range(together)]
+        first, last = [], []
+        for step in range(steps):
+            first.append(jnp.minimum(begins[step] // together, rounds - 1))
+            last.append(jnp.maximum(first[step], (ends[step] + together - 1) // together - 1))
+        for step in range(steps):
+
+            @pl.when(first[step] == turn)
+            def _():
+                for copy in vel_in(step):
+                    copy.wait()
+
+        for spot, source in found:
+            add_source(spot, source)
+        for step in range(steps):
+
+            @pl.when(last[step] == turn)
+            def _():
+                for copy in vel_copy(step):
+                    copy.start()
+
         return 0
 
-    lax.fori_loop(0, members * CAP, add_source, 0)
+    lax.fori_loop(0, rounds, one_round, 0)
     for step in range(steps):
-        vel_copy(step).start()
-    for step in range(steps):
-        vel_copy(step).wait()
+        for copy in vel_copy(step):
+            copy.wait()
 
 
 def add_drag(block_ids, owners, parcels, sampled, velocity):
     _, nx, ny, nz = velocity.shape
     members = parcels.shape[0]
     slots = members * CAP
+    steps = nx // EDGE
+    hbm, vmem = pl.BlockSpec(memory_space=pltpu.HBM), pl.BlockSpec(memory_space=pltpu.VMEM)
     return pl.pallas_call(
         functools.partial(source_body, ny // EDGE, nz // EDGE),
-        in_specs=[pl.BlockSpec(memory_space=pltpu.SMEM)] * 2
-        + [pl.BlockSpec(memory_space=pltpu.VMEM)] * 2
-        + [pl.BlockSpec(memory_space=pltpu.HBM)],
-        out_specs=pl.BlockSpec(memory_space=pltpu.HBM),
+        in_specs=[hbm, hbm, vmem, vmem, hbm],
+        out_specs=hbm,
         out_shape=jax.ShapeDtypeStruct(velocity.shape, BF16),
         scratch_shapes=[
+            pltpu.SMEM(block_ids.shape, jnp.int32),
+            pltpu.SMEM(owners.shape, jnp.int32),
             pltpu.SMEM((slots,), jnp.int32),
             pltpu.SMEM((members,), jnp.int32),
+            pltpu.SMEM((slots,), jnp.int32),
+            pltpu.SMEM((steps,), jnp.int32),
+            pltpu.SMEM((steps,), jnp.int32),
             pltpu.VMEM(velocity.shape, BF16),
-            pltpu.VMEM((slots, EDGE * EDGE, 3 * LANES), BF16),
-            pltpu.SemaphoreType.DMA((2, nx // EDGE)),
+            pltpu.SemaphoreType.DMA((6, steps)),
+            pltpu.SemaphoreType.DMA((2,)),
         ],
         compiler_params=params(),
         name="add_drag",
-    )(block_ids, owners, parcels, sampled, *in_hbm(velocity))
+    )(*in_hbm(block_ids, owners), parcels, sampled, *in_hbm(velocity))
 
 
 def drag_body(vel_ref, rate_ref, sampled_ref, out_ref):
@@ -552,9 +631,9 @@
         below_x, above_x, below_y, above_y, rate.shape[0],
     )
     parcels_in, windows = lax.optimization_barrier((parcels_in, windows))
-    sampled = sample_parcels(block_ids, owners, parcels_in, windows)
+    sampled, kept = sample_parcels(parcels_in, windows)
     returned = lax.all_to_all(sampled, "member", split_axis=0, concat_axis=0, tiled=True)
-    velocity_next = add_drag(block_ids, owners, parcels_in, sampled, velocity)
+    velocity_next = add_drag(block_ids, owners, parcels_in, kept, velocity)
     vel_next = drag(vel, rate, returned)
     parcel_next = jnp.swapaxes(vel_next, 1, 2)[None, None]
     return (frac_next, velocity_next, parcel_next)

time: 45.1 us -> 38.7 us (0.86)
  waiting for transfers between devices: 3.08 us -> 0.18 us
  Pallas kernels: 22.4 us -> 20.2 us
  starting transfers between devices: 18.5 us -> 17 us
    all_to_all x1, starting transfers between devices: 7.25 us -> 3.39 us  [per_device(): lax.all_to_all(parcels, 'member', split_axis=0, concat_axis=0, tiled=True)]
    ppermute x4, waiting for transfers between devices: 3.07 us -> 0.01 us  [passed_around(): lax.ppermute(block, axis, [(i, (i + distance) % size) for i in range(size)])]
    pallas_call x1, Pallas kernels: 8.02 us -> 6.72 us  [add_drag(): pl.pallas_call(functools.partial(source_body, ny // EDGE, nz // EDGE), in...]
    ppermute x4, starting transfers between devices: 6.46 us -> 7.72 us  [passed_around(): lax.ppermute(block, axis, [(i, (i + distance) % size) for i in range(size)])]
    all_to_all x1, starting transfers between devices: 4.75 us -> 5.92 us  [per_device(): lax.all_to_all(sampled, 'member', split_axis=0, concat_axis=0, tiled=True)]
    pallas_call x1, Pallas kernels: 2.74 us -> 1.67 us  [sample_parcels(): pl.pallas_call(sample_body, in_specs=[pl.BlockSpec(memory_space=pltpu.VME...]
  transfers between devices with their start and end apart: 6 -> 6, of which waited for: 2 -> 1; matrix products, arithmetic and copies ran while one was open for 0% -> 0% of each run, Pallas kernels for 37% -> 41%
where the time goes in v3:
time: 38.7 us; the launch traced here: 38.2 us
  Pallas kernels  20.2 us (52%)
  starting transfers between devices  17 us (44%)
  between operations  0.7 us (2%)
    pallas_call x1, Pallas kernels, advect(): pl.pallas_call(functools.partial(advect_body, ny // EDGE, nz // EDGE), in...  8.82 us
    ppermute x4, starting transfers between devices, passed_around(): lax.ppermute(block, axis, [(i, (i + distance) % size) for i in range(size)])  7.72 us
    pallas_call x1, Pallas kernels, add_drag(): pl.pallas_call(functools.partial(source_body, ny // EDGE, nz // EDGE), in...  6.72 us
    all_to_all x1, starting transfers between devices, per_device(): lax.all_to_all(sampled, 'member', split_axis=0, concat_axis=0, tiled=True)  5.92 us
    all_to_all x1, starting transfers between devices, per_device(): lax.all_to_all(parcels, 'member', split_axis=0, concat_axis=0, tiled=True)  3.39 us
    pallas_call x1, Pallas kernels, pack(): pl.pallas_call(pack_body, grid=(1,), in_specs=[whole(vel.shape), whole(ra...  2.25 us
    pallas_call x1, Pallas kernels, sample_parcels(): pl.pallas_call(sample_body, in_specs=[pl.BlockSpec(memory_space=pltpu.VME...  1.67 us
  transfers between devices with their start and end apart: 6, of which 1 were waited for; matrix products, arithmetic and copies ran while one was open for 0% of the time, Pallas kernels for 41%

profile of v3, /device:TPU:0, one launch (start us, length us, event | category | flops | bytes accessed | tf_op | source)
XLA Modules:
  0.0 38.2 jit_solution(7052127945246662070)
XLA Ops:
  0.6 2.3 %pack.1 = (f32[8,6,2,512]{3,2,1,0:T(2,128)}, bf16[2,64,256]{2,1,0:T(8,128)(2,1)S(1)}, bf16[1,64,256]{2,1,0:T(8,128)(2,1)S(1)}, bf16[2,64,256]{2,1,0:T(8,128)(2,1)S(1)}, bf16[1,64,256]{2,1,0:T(8,128)(2,1)S(1)}) custom-call(f32[8,3,2,512]{3,2,1,0:T(2,128)} %bitcast.15, f32[8,2,512]{2,1,0:T(2,128)} %bitcast.17, f32[8,2,512]{2,1,0:T(2,128)} %bitcast.20, ...), custom_call_target="tpu_custom_call" | custom-call | tf_op jit(solution)/shard_map/pack/pallas_call | solution.py:55
  2.9 0.5 %collective-permute-start = (bf16[2,64,256]{2,1,0:T(8,128)(2,1)S(1)}, bf16[2,64,256]{2,1,0:T(8,128)(2,1)S(1)}, u32[]{:S(2)}, u32[]{:S(2)}) collective-permute-start(bf16[2,64,256]{2,1,0:T(8,128)(2,1)S(1)} %get-tuple-element.14), channel_id=1, source_target_pairs={{0,8},{8,16},{16,24},{24,0},{1,9},{9,17},{17,25},{25,1},{2,10},{10... | collective-permute-start | bytes 196616 | tf_op jit(solution)/shard_map/ppermute | solution.py:24
  3.3 2.0 %collective-permute-start.1 = (bf16[1,64,256]{2,1,0:T(8,128)(2,1)S(1)}, bf16[1,64,256]{2,1,0:T(8,128)(2,1)S(1)}, u32[]{:S(2)}, u32[]{:S(2)}) collective-permute-start(bf16[1,64,256]{2,1,0:T(8,128)(2,1)S(1)} %get-tuple-element.15), channel_id=1, source_target_pairs={{0,24},{8,0},{16,8},{24,16},{1,25},{9,1},{17,9},{25,17},{2,26},{10... | collective-permute-start | bytes 98312 | tf_op jit(solution)/shard_map/ppermute | solution.py:24
  5.3 2.3 %collective-permute-start.2 = (bf16[2,64,256]{2,1,0:T(8,128)(2,1)S(1)}, bf16[2,64,256]{2,1,0:T(8,128)(2,1)S(1)}, u32[]{:S(2)}, u32[]{:S(2)}) collective-permute-start(bf16[2,64,256]{2,1,0:T(8,128)(2,1)S(1)} %get-tuple-element.16), channel_id=1, source_target_pairs={{0,1},{1,2},{2,3},{3,4},{4,5},{5,6},{6,7},{7,0},{8,9},{9,10},{10,1... | collective-permute-start | bytes 196616 | tf_op jit(solution)/shard_map/ppermute | solution.py:24
  7.6 3.0 %collective-permute-start.3 = (bf16[1,64,256]{2,1,0:T(8,128)(2,1)S(1)}, bf16[1,64,256]{2,1,0:T(8,128)(2,1)S(1)}, u32[]{:S(2)}, u32[]{:S(2)}) collective-permute-start(bf16[1,64,256]{2,1,0:T(8,128)(2,1)S(1)} %get-tuple-element.17), channel_id=1, source_target_pairs={{0,7},{1,0},{2,1},{3,2},{4,3},{5,4},{6,5},{7,6},{8,15},{9,8},{10,9... | collective-permute-start | bytes 98312 | tf_op jit(solution)/shard_map/ppermute | solution.py:24
  10.6 3.4 %all-to-all-start = ((f32[8,6,2,512]{3,2,1,0:T(2,128)}), f32[8,6,2,512]{3,2,1,0:T(2,128)S(1)}, u32[]{:S(2)}, u32[]{:S(2)}) async-start(f32[8,6,2,512]{3,2,1,0:T(2,128)} %get-tuple-element.19), calls=%async_computation | async-start | bytes 393216 | tf_op jit(solution)/shard_map/all_to_all | solution.py:620
  14.0 0.1 add_convert_fusion.edge_sm
  14.1 0.0 collective-permute-done.1.halo_above_x
  14.1 0.0 collective-permute-done.3.halo_above_y
  14.1 0.0 collective-permute-done.halo_below_x
  14.1 0.0 collective-permute-done.2.halo_below_y
  14.1 8.8 %advect.1 = (f32[64,64,256]{2,1,0:T(8,128)}, bf16[16,64,256]{2,1,0:T(8,128)(2,1)S(1)}) custom-call(s32[16]{0:T(128)} %bitcast.22, s32[16]{0:T(128)} %bitcast.24, s32[4]{0:T(128)S(1)} %add_convert_fusion.edge_sm, bf16[2,64,256]{2,1,0:T(8,128)(2,1)S(1)} %collective-permute-done.halo_below_x, bf16[1,64,256]{2,1,0:T(8,128)(2,1)S(1)} %collective-permute-done.1.halo_above_x, ...), custom_call_target="tpu_custom_call" | custom-call | flops 9093251072 | bytes 117440512 | tf_op jit(solution)/shard_map/advect/pallas_call | solution.py:326
  23.0 0.0 all-to-all-done.parcels_ref
  23.0 1.7 %sample.1 = (bf16[8,8,512]{2,1,0:T(8,128)(2,1)}, bf16[8,8,512]{2,1,0:T(8,128)(2,1)S(1)}) custom-call(f32[8,6,2,512]{3,2,1,0:T(2,128)S(1)} %all-to-all-done.parcels_ref, bf16[16,64,256]{2,1,0:T(8,128)(2,1)S(1)} %get-tuple-element.22.windows_ref), custom_call_target="tpu_custom_call" | custom-call | tf_op jit(solution)/shard_map/sample/pallas_call | solution.py:407
  24.6 5.9 %all-to-all-start.1 = ((bf16[8,8,512]{2,1,0:T(8,128)(2,1)}), bf16[8,8,512]{2,1,0:T(8,128)(2,1)S(1)}, u32[]{:S(2)}, u32[]{:S(2)}) async-start(bf16[8,8,512]{2,1,0:T(8,128)(2,1)} %get-tuple-element.24), calls=%async_computation.1 | async-start | bytes 131072 | tf_op jit(solution)/shard_map/all_to_all | solution.py:635
  30.6 0.0 copy-start
  30.6 0.0 copy-start.1
  30.6 6.7 %add_drag.1 = bf16[3,64,64,256]{3,2,1,0:T(8,128)(2,1)} custom-call(s32[16]{0:T(128)} %bitcast.23, s32[16]{0:T(128)} %bitcast.25, f32[8,6,2,512]{3,2,1,0:T(2,128)S(1)} %all-to-all-done.parcels_ref, bf16[8,8,512]{2,1,0:T(8,128)(2,1)S(1)} %get-tuple-element.23.sampled_ref, bf16[3,64,64,256]{3,2,1,0:T(8,128)(2,1)} %vel_hbm.3), custom_call_target="tpu_custom_call" | custom-call | tf_op jit(solution)/shard_map/add_drag/pallas_call | solution.py:558
  37.3 0.2 all-to-all-done.1.sampled_ref
  37.5 0.0 copy-done
  37.5 0.0 copy-done.1
  37.5 0.7 %drag.1 = f32[8,3,2,512]{3,2,1,0:T(2,128)} custom-call(f32[8,3,2,512]{3,2,1,0:T(2,128)S(1)} %bitcast.16, f32[8,2,512]{2,1,0:T(2,128)S(1)} %bitcast.18, bf16[8,8,512]{2,1,0:T(8,128)(2,1)S(1)} %all-to-all-done.1.sampled_ref), custom_call_target="tpu_custom_call" | custom-call | tf_op jit(solution)/shard_map/drag/pallas_call | solution.py:591
Async XLA Ops:
  2.9 11.2 %collective-permute-start = (bf16[2,64,256]{2,1,0:T(8,128)(2,1)S(1)}, bf16[2,64,256]{2,1,0:T(8,128)(2,1)S(1)}, u32[]{:S(2)}, u32[]{:S(2)}) collective-permute-start(bf16[2,64,256]{2,1,0:T(8,128)(2,1)S(1)} %get-tuple-element.14), channel_id=1, source_target_pairs={{0,8},{8,16},{16,24},{24,0},{1,9},{9,17},{17,25},{25,1},{2,10},{10... | collective-permute-start | bytes 196616 | tf_op jit(solution)/shard_map/ppermute | solution.py:24
  3.3 10.8 %collective-permute-start.1 = (bf16[1,64,256]{2,1,0:T(8,128)(2,1)S(1)}, bf16[1,64,256]{2,1,0:T(8,128)(2,1)S(1)}, u32[]{:S(2)}, u32[]{:S(2)}) collective-permute-start(bf16[1,64,256]{2,1,0:T(8,128)(2,1)S(1)} %get-tuple-element.15), channel_id=1, source_target_pairs={{0,24},{8,0},{16,8},{24,16},{1,25},{9,1},{17,9},{25,17},{2,26},{10... | collective-permute-start | bytes 98312 | tf_op jit(solution)/shard_map/ppermute | solution.py:24
  5.3 8.8 %collective-permute-start.2 = (bf16[2,64,256]{2,1,0:T(8,128)(2,1)S(1)}, bf16[2,64,256]{2,1,0:T(8,128)(2,1)S(1)}, u32[]{:S(2)}, u32[]{:S(2)}) collective-permute-start(bf16[2,64,256]{2,1,0:T(8,128)(2,1)S(1)} %get-tuple-element.16), channel_id=1, source_target_pairs={{0,1},{1,2},{2,3},{3,4},{4,5},{5,6},{6,7},{7,0},{8,9},{9,10},{10,1... | collective-permute-start | bytes 196616 | tf_op jit(solution)/shard_map/ppermute | solution.py:24
  7.6 6.5 %collective-permute-start.3 = (bf16[1,64,256]{2,1,0:T(8,128)(2,1)S(1)}, bf16[1,64,256]{2,1,0:T(8,128)(2,1)S(1)}, u32[]{:S(2)}, u32[]{:S(2)}) collective-permute-start(bf16[1,64,256]{2,1,0:T(8,128)(2,1)S(1)} %get-tuple-element.17), channel_id=1, source_target_pairs={{0,7},{1,0},{2,1},{3,2},{4,3},{5,4},{6,5},{7,6},{8,15},{9,8},{10,9... | collective-permute-start | bytes 98312 | tf_op jit(solution)/shard_map/ppermute | solution.py:24
  10.6 12.3 %all-to-all-start = ((f32[8,6,2,512]{3,2,1,0:T(2,128)}), f32[8,6,2,512]{3,2,1,0:T(2,128)S(1)}, u32[]{:S(2)}, u32[]{:S(2)}) async-start(f32[8,6,2,512]{3,2,1,0:T(2,128)} %get-tuple-element.19), calls=%async_computation | async-start | bytes 393216 | tf_op jit(solution)/shard_map/all_to_all | solution.py:620
  24.6 12.8 %all-to-all-start.1 = ((bf16[8,8,512]{2,1,0:T(8,128)(2,1)}), bf16[8,8,512]{2,1,0:T(8,128)(2,1)S(1)}, u32[]{:S(2)}, u32[]{:S(2)}) async-start(bf16[8,8,512]{2,1,0:T(8,128)(2,1)} %get-tuple-element.24), calls=%async_computation.1 | async-start | bytes 131072 | tf_op jit(solution)/shard_map/all_to_all | solution.py:635
  30.6 6.9 %copy-start = (f32[1,1,8,2,3,512]{5,3,4,2,1,0:T(2,128)S(1)}, f32[1,1,8,2,3,512]{5,3,4,2,1,0:T(2,128)}, u32[]{:S(2)}) copy-start(f32[1,1,8,2,3,512]{5,3,4,2,1,0:T(2,128)} %param.12) | copy-start | bytes 294916
  30.6 6.9 %copy-start.1 = (f32[1,1,8,2,512]{4,3,2,1,0:T(2,128)S(1)}, f32[1,1,8,2,512]{4,3,2,1,0:T(2,128)}, u32[]{:S(2)}) copy-start(f32[1,1,8,2,512]{4,3,2,1,0:T(2,128)} %param.13) | copy-start | bytes 98308

commit v4 on v3

--- a/solution.py
+++ b/solution.py
@@ -33,20 +33,48 @@
 
 
 def pack_body(
-    vel_ref, rate_ref, weight_ref, cell_ref,
-    f_first_x, f_last_x, u_last_x, f_first_y, f_last_y, u_last_y,
-    parcels_ref, up_x, down_x, up_y, down_y,
+    vel_hbm, rate_hbm, weight_hbm, cell_hbm, frac_hbm, velocity_hbm,
+    parcels_hbm, up_x, down_x, up_y, down_y,
+    cells, staged, f_first_x, f_last_x, u_last_x, f_first_y, f_last_y, u_last_y, sems,
 ):
-    parcels_ref[:, 0:3] = vel_ref[...]
-    parcels_ref[:, 3] = rate_ref[...]
-    parcels_ref[:, 4] = weight_ref[...]
-    parcels_ref[:, 5] = cell_ref[...].astype(F32)
-    up_x[0] = f_last_x[0].astype(BF16)
-    up_x[1] = u_last_x[0, 0]
-    down_x[0] = f_first_x[0].astype(BF16)
+    nx, ny, nz = frac_hbm.shape
+    cells_in = pltpu.make_async_copy(cell_hbm, cells, sems.at[0])
+    straight = [
+        pltpu.make_async_copy(vel_hbm, staged.at[:, 0:3], sems.at[1]),
+        pltpu.make_async_copy(rate_hbm, staged.at[:, 3], sems.at[2]),
+        pltpu.make_async_copy(weight_hbm, staged.at[:, 4], sems.at[3]),
+    ]
+    staged_out = pltpu.make_async_copy(staged, parcels_hbm, sems.at[4])
+    pieces = [
+        pltpu.make_async_copy(source, piece, sems.at[5 + i])
+        for i, (source, piece) in enumerate(
+            [
+                (frac_hbm.at[:, pl.ds(0, 8)], f_first_y),
+                (frac_hbm.at[:, pl.ds(ny - 8, 8)], f_last_y),
+                (velocity_hbm.at[1, :, pl.ds(ny - 16, 16)], u_last_y),
+                (frac_hbm.at[0], f_first_x),
+                (frac_hbm.at[nx - 1], f_last_x),
+                (velocity_hbm.at[0, nx - 1], u_last_x),
+            ]
+        )
+    ]
+    cells_in.start()
+    for copy in straight + pieces:
+        copy.start()
+    cells_in.wait()
+    staged[:, 5] = cells[...].astype(F32)
+    for copy in straight:
+        copy.wait()
+    staged_out.start()
+    for copy in pieces:
+        copy.wait()
+    up_x[0] = f_last_x[...].astype(BF16)
+    up_x[1] = u_last_x[...]
+    down_x[0] = f_first_x[...].astype(BF16)
     up_y[0] = f_last_y[:, 7, :].astype(BF16)
-    up_y[1] = u_last_y[0].astype(F32)[:, 15, :].astype(BF16)
+    up_y[1] = u_last_y[...].astype(F32)[:, 15, :].astype(BF16)
     down_y[0] = f_first_y[:, 0, :].astype(BF16)
+    staged_out.wait()
 
 
 def pack(volume_frac, velocity, vel, rate, weight, cell):
@@ -54,26 +82,9 @@
     members, _, parcels = rate.shape
     return pl.pallas_call(
         pack_body,
-        grid=(1,),
-        in_specs=[
-            whole(vel.shape),
-            whole(rate.shape),
-            whole(weight.shape),
-            whole(cell.shape),
-            pl.BlockSpec((1, ny, nz), lambda i: (0, 0, 0)),
-            pl.BlockSpec((1, ny, nz), lambda i: (nx - 1, 0, 0)),
-            pl.BlockSpec((1, 1, ny, nz), lambda i: (0, nx - 1, 0, 0)),
-            pl.BlockSpec((nx, 8, nz), lambda i: (0, 0, 0)),
-            pl.BlockSpec((nx, 8, nz), lambda i: (0, ny // 8 - 1, 0)),
-            pl.BlockSpec((1, nx, 16, nz), lambda i: (1, 0, ny // 16 - 1, 0)),
-        ],
-        out_specs=[
-            whole((members, FIELDS, CAP, parcels)),
-            whole((2, ny, nz)),
-            whole((1, ny, nz)),
-            whole((2, nx, nz)),
-            whole((1, nx, nz)),
-        ],
+        in_specs=[pl.BlockSpec(memory_space=pltpu.HBM)] * 6,
+        out_specs=[pl.BlockSpec(memory_space=pltpu.HBM)]
+        + [pl.BlockSpec(memory_space=pltpu.VMEM)] * 4,
         out_shape=[
             jax.ShapeDtypeStruct((members, FIELDS, CAP, parcels), F32),
             jax.ShapeDtypeStruct((2, ny, nz), BF16),
@@ -81,41 +92,69 @@
             jax.ShapeDtypeStruct((2, nx, nz), BF16),
             jax.ShapeDtypeStruct((1, nx, nz), BF16),
         ],
+        scratch_shapes=[
+            pltpu.VMEM(cell.shape, jnp.int32),
+            pltpu.VMEM((members, FIELDS, CAP, parcels), F32),
+            pltpu.VMEM((ny, nz), F32),
+            pltpu.VMEM((ny, nz), F32),
+            pltpu.VMEM((ny, nz), BF16),
+            pltpu.VMEM((nx, 8, nz), F32),
+            pltpu.VMEM((nx, 8, nz), F32),
+            pltpu.VMEM((nx, 16, nz), BF16),
+            pltpu.SemaphoreType.DMA((11,)),
+        ],
         compiler_params=params(),
         name="pack",
-    )(
-        *in_hbm(vel, rate, weight, cell),
-        *in_hbm(volume_frac, volume_frac, velocity, volume_frac, volume_frac, velocity),
-    )
-
-
-def slot_table(block_sm, owner_sm, table, count, drops, members):
-    def clear_count(i, _):
-        count[i] = 0
-        return 0
-
-    def clear_table(i, _):
-        table[i] = -1
-        return 0
-
-    lax.fori_loop(0, members, clear_count, 0)
-    lax.fori_loop(0, members * CAP, clear_table, 0)
-
-    def enter(j, _):
+    )(*in_hbm(vel, rate, weight, cell, volume_frac, velocity))
+
+
+def slot_table(block_sm, owner_sm, table):
+    for slot in range(table.shape[0]):
+        table[slot] = -1
+    owners = []
+    for j in range(block_sm.shape[0]):
         owner = owner_sm[j]
-        place = count[owner]
-        count[owner] = place + 1
+        place = 0
+        for earlier in owners:
+            place = place + (earlier == owner).astype(jnp.int32)
+        owners.append(owner)
         table[owner * CAP + place] = block_sm[j]
-        return 0
-
-    lax.fori_loop(0, drops, enter, 0)
+
+
+def slots_by_slab(table, order, steps, blocks_in_slab):
+    slabs = [
+        parted(jnp.maximum(table[slot], 0), blocks_in_slab)[0] for slot in range(order.shape[0])
+    ]
+    begins, ends = [], []
+    at = 0
+    for step in range(steps):
+        begins.append(at)
+        for slab in slabs:
+            at = at + (slab == step).astype(jnp.int32)
+        ends.append(at)
+    following = list(begins)
+    for slot, slab in enumerate(slabs):
+        spot = following[0]
+        for step in range(1, steps):
+            spot = jnp.where(slab == step, following[step], spot)
+        order[spot] = slot
+        for step in range(steps):
+            following[step] = following[step] + (slab == step).astype(jnp.int32)
+    return begins, ends
+
+
+def parted(number, size):
+    if size & (size - 1) == 0:
+        return lax.shift_right_logical(number, size.bit_length() - 1), jnp.bitwise_and(number, size - 1)
+    return number // size, number % size
 
 
 def corner(block, blocks_y, blocks_z):
-    x = block // (blocks_y * blocks_z) * EDGE
-    y = pl.multiple_of(block // blocks_z % blocks_y * EDGE, EDGE)
-    z = block % blocks_z * EDGE
-    return x, y, pl.multiple_of(z // LANES * LANES, LANES), z % LANES
+    upper, bz = parted(block, blocks_z)
+    bx, by = parted(upper, blocks_y)
+    tile, place = parted(bz, LANES // EDGE)
+    x = bx * EDGE
+    return x, pl.multiple_of(by * EDGE, EDGE), pl.multiple_of(tile * LANES, LANES), place * EDGE
 
 
 def rows_of_cell(cell):
@@ -142,14 +181,12 @@
 
 def advect_body(
     blocks_y, blocks_z,
-    block_hbm, owner_hbm, edge_sm,
+    block_hbm, owner_hbm,
     halo_below_x, halo_above_x, halo_below_y, halo_above_y, frac_hbm, vel_hbm,
     frac_next, windows_ref,
-    block_sm, owner_sm, table, count, frac_ref, vel_ref, frac_out, sides, flux_low,
+    block_sm, owner_sm, table, frac_ref, vel_ref, frac_out, sides, flux_low,
     right_even, right_odd, third_even, third_odd, rest_even, rest_odd, sems, scalar_sems,
 ):
-    members = count.shape[0]
-    drops = block_sm.shape[0]
     nx, ny, nz = frac_out.shape
     steps = sems.shape[1]
     depth = nx // steps
@@ -176,6 +213,12 @@
             frac_out.at[part(step)], frac_next.at[part(step)], sems.at[1, step]
         )
 
+    scalars = [
+        pltpu.make_async_copy(block_hbm, block_sm, scalar_sems.at[0]),
+        pltpu.make_async_copy(owner_hbm, owner_sm, scalar_sems.at[1]),
+    ]
+    for copy in scalars:
+        copy.start()
     frac_in(0).start()
     for step in range(steps):
         for copy in vel_in(step):
@@ -183,17 +226,11 @@
         if step + 1 < steps:
             frac_in(step + 1).start()
 
-    scalars = [
-        pltpu.make_async_copy(block_hbm, block_sm, scalar_sems.at[0]),
-        pltpu.make_async_copy(owner_hbm, owner_sm, scalar_sems.at[1]),
-    ]
-    for copy in scalars:
-        copy.start()
-    for copy in scalars:
-        copy.wait()
-    slot_table(block_sm, owner_sm, table, count, drops, members)
-
-    inner = [edge_sm[i].astype(F32) for i in range(4)]
+
+    inner = []
+    for axis in ("group", "member"):
+        at, size = lax.axis_index(axis), lax.axis_size(axis)
+        inner += [(at > 0).astype(F32), (at < size - 1).astype(F32)]
     frac_ref[nx] = halo_above_x[0].astype(F32) * inner[1]
     sides[0:2] = halo_below_y[...].astype(F32) * inner[2]
     sides[2:3] = halo_above_y[...].astype(F32) * inner[3]
@@ -267,7 +304,27 @@
     total = nx // chunk
     look_right(0, right_even)
 
+    nothing = jnp.where(
+        lax.broadcasted_iota(jnp.int32, (4 * EDGE, EDGE * EDGE), 0) >= 3 * EDGE, 1.0, 0.0
+    ).astype(BF16)
+    together = GROUP * CAP
+
+    def some_windows(turn, _):
+        for more in range(together):
+            slot = turn * together + more
+            x, y, z, shift = corner(jnp.maximum(table[slot], 0), blocks_y, blocks_z)
+            spot = (pl.ds(x, EDGE), pl.ds(y, EDGE), pl.ds(z, LANES))
+            window = window_of(shift, vel_ref, frac_ref, spot)
+            windows_ref[slot] = jnp.where(table[slot] >= 0, window, nothing)
+        return 0
+
     def one_step(step, _):
+        @pl.when(step == 1)
+        def _():
+            for copy in scalars:
+                copy.wait()
+            slot_table(block_sm, owner_sm, table)
+
         for copy in vel_in(step):
             copy.wait()
 
@@ -294,21 +351,8 @@
     lax.fori_loop(0, steps, one_step, 0)
     finish(total - 1, third_odd, rest_odd)
     frac_copy(steps - 1).start()
-
-    nothing = jnp.where(
-        lax.broadcasted_iota(jnp.int32, (4 * EDGE, EDGE * EDGE), 0) >= 3 * EDGE, 1.0, 0.0
-    ).astype(BF16)
-
-    def some_windows(first, _):
-        for more in range(GROUP * CAP):
-            slot = first * GROUP * CAP + more
-            x, y, z, shift = corner(jnp.maximum(table[slot], 0), blocks_y, blocks_z)
-            spot = (pl.ds(x, EDGE), pl.ds(y, EDGE), pl.ds(z, LANES))
-            window = window_of(shift, vel_ref, frac_ref, spot)
-            windows_ref[slot] = jnp.where(table[slot] >= 0, window, nothing)
-        return 0
-
-    lax.fori_loop(0, members // GROUP, some_windows, 0)
+    for turn in range(table.shape[0] // together):
+        some_windows(turn, 0)
 
     for step in range(steps):
         frac_copy(step).wait()
@@ -318,7 +362,7 @@
     return [pltpu.with_memory_space_constraint(array, pltpu.HBM) for array in arrays]
 
 
-def advect(block_ids, owners, edges, volume_frac, velocity, below_x, above_x, below_y, above_y, members):
+def advect(block_ids, owners, volume_frac, velocity, below_x, above_x, below_y, above_y, members):
     nx, ny, nz = volume_frac.shape
     slots = members * CAP
     steps = nx // 8
@@ -326,7 +370,6 @@
     return pl.pallas_call(
         functools.partial(advect_body, ny // EDGE, nz // EDGE),
         in_specs=[pl.BlockSpec(memory_space=pltpu.HBM)] * 2
-        + [pl.BlockSpec(memory_space=pltpu.SMEM)]
         + [pl.BlockSpec(memory_space=pltpu.VMEM)] * 4
         + [pl.BlockSpec(memory_space=pltpu.HBM)] * 2,
         out_specs=[
@@ -341,7 +384,6 @@
             pltpu.SMEM(block_ids.shape, jnp.int32),
             pltpu.SMEM(owners.shape, jnp.int32),
             pltpu.SMEM((slots,), jnp.int32),
-            pltpu.SMEM((members,), jnp.int32),
             pltpu.VMEM((nx + 1, ny, nz), F32),
             pltpu.VMEM(velocity.shape, BF16),
             pltpu.VMEM(volume_frac.shape, F32),
@@ -364,7 +406,7 @@
         ),
         name="advect",
     )(
-        *in_hbm(block_ids, owners), edges, below_x, above_x, below_y, above_y,
+        *in_hbm(block_ids, owners), below_x, above_x, below_y, above_y,
         *in_hbm(volume_frac, velocity),
     )
 
@@ -417,7 +459,7 @@
 def source_body(
     blocks_y, blocks_z, block_hbm, owner_hbm, parcels_ref, sampled_ref, vel_hbm,
     vel_next,
-    block_sm, owner_sm, table, count, order, begins, ends, vel_ref, sems, scalar_sems,
+    block_sm, owner_sm, table, order, vel_ref, sems, scalar_sems,
 ):
     members = parcels_ref.shape[0]
     parcels = parcels_ref.shape[-1]
@@ -455,29 +497,14 @@
             copy.start()
     for copy in scalars:
         copy.wait()
-    slot_table(block_sm, owner_sm, table, count, block_sm.shape[0], members)
-
-    filled = 0
-    for step in range(steps):
-        begins[step] = filled
-
-        def enter(slot, at):
-            mine = jnp.maximum(table[slot], 0) // (blocks_y * blocks_z) == step
-
-            @pl.when(mine)
-            def _():
-                order[at] = slot
-
-            return at + mine.astype(jnp.int32)
-
-        filled = lax.fori_loop(0, slots, enter, filled)
-        ends[step] = filled
+    slot_table(block_sm, owner_sm, table)
+    begins, ends = slots_by_slab(table, order, steps, blocks_y * blocks_z)
 
     def source_of(slot):
         block = table[slot]
         spot = corner(jnp.maximum(block, 0), blocks_y, blocks_z)
-        member = slot // CAP
-        odd = slot % CAP == 1
+        member, place = parted(slot, CAP)
+        odd = place == 1
         both = [parcels_ref[member, k] for k in range(FIELDS)]
         field = [jnp.where(odd, value[1:2], value[0:1]) for value in both]
         got = sampled_ref[member].astype(F32)
@@ -519,12 +546,18 @@
             here = (k, pl.ds(x, EDGE), pl.ds(y, EDGE), pl.ds(z, LANES))
             vel_ref[here] = vel_ref[here] + source[k].reshape(EDGE, EDGE, LANES)
 
-    def one_round(turn, _):
-        found = [source_of(order[turn * together + more]) for more in range(together)]
-        first, last = [], []
-        for step in range(steps):
-            first.append(jnp.minimum(begins[step] // together, rounds - 1))
-            last.append(jnp.maximum(first[step], (ends[step] + together - 1) // together - 1))
+    first, last = [], []
+    for step in range(steps):
+        first.append(jnp.minimum(parted(begins[step], together)[0], rounds - 1))
+        last.append(
+            jnp.maximum(first[step], parted(ends[step] + together - 1, together)[0] - 1)
+        )
+
+    def sources_of(turn):
+        return [source_of(order[turn * together + more]) for more in range(together)]
+
+    found = sources_of(0)
+    for turn in range(rounds):
         for step in range(steps):
 
             @pl.when(first[step] == turn)
@@ -532,8 +565,10 @@
                 for copy in vel_in(step):
                     copy.wait()
 
+        following = sources_of(turn + 1) if turn + 1 < rounds else None
         for spot, source in found:
             add_source(spot, source)
+        found = following
         for step in range(steps):
 
             @pl.when(last[step] == turn)
@@ -541,9 +576,6 @@
                 for copy in vel_copy(step):
                     copy.start()
 
-        return 0
-
-    lax.fori_loop(0, rounds, one_round, 0)
     for step in range(steps):
         for copy in vel_copy(step):
             copy.wait()
@@ -564,10 +596,7 @@
             pltpu.SMEM(block_ids.shape, jnp.int32),
             pltpu.SMEM(owners.shape, jnp.int32),
             pltpu.SMEM((slots,), jnp.int32),
-            pltpu.SMEM((members,), jnp.int32),
             pltpu.SMEM((slots,), jnp.int32),
-            pltpu.SMEM((steps,), jnp.int32),
-            pltpu.SMEM((steps,), jnp.int32),
             pltpu.VMEM(velocity.shape, BF16),
             pltpu.SemaphoreType.DMA((6, steps)),
             pltpu.SemaphoreType.DMA((2,)),
@@ -618,16 +647,8 @@
     below_y = passed_around(up_y, "member", 1)
     above_y = passed_around(down_y, "member", -1)
     parcels_in = lax.all_to_all(parcels, "member", split_axis=0, concat_axis=0, tiled=True)
-    edges = jnp.stack(
-        [
-            lax.axis_index("group") > 0,
-            lax.axis_index("group") < lax.axis_size("group") - 1,
-            lax.axis_index("member") > 0,
-            lax.axis_index("member") < lax.axis_size("member") - 1,
-        ]
-    ).astype(jnp.int32)
     frac_next, windows = advect(
-        block_ids, owners, edges, volume_frac, velocity,
+        block_ids, owners, volume_frac, velocity,
         below_x, above_x, below_y, above_y, rate.shape[0],
     )
     parcels_in, windows = lax.optimization_barrier((parcels_in, windows))

time: 38.7 us -> 37.6 us (0.972)
  Pallas kernels: 20.2 us -> 18.3 us
  waiting for transfers between devices: 0.18 us -> 1.11 us
    all_to_all x1, waiting for transfers between devices: 0.16 us -> 1.09 us  [per_device(): lax.all_to_all(sampled, 'member', split_axis=0, concat_axis=0, tiled=True)]
    pallas_call x1, Pallas kernels: 6.72 us -> 5.79 us  [add_drag(): pl.pallas_call(functools.partial(source_body, ny // EDGE, nz // EDGE), in...]
    pallas_call x1, Pallas kernels: 8.82 us -> 8.35 us  [advect(): pl.pallas_call(functools.partial(advect_body, ny // EDGE, nz // EDGE), in...]
    pallas_call x1, Pallas kernels: 2.25 us -> 1.79 us  [pack(): pl.pallas_call(pack_body, in_specs=[pl.BlockSpec(memory_space=pltpu.HBM)]...]
  transfers between devices with their start and end apart: 6 -> 6, of which waited for: 1 -> 1; matrix products, arithmetic and copies ran while one was open for 0% -> 0% of each run, Pallas kernels for 41% -> 38%
where the time goes in v4:
time: 37.6 us; the launch traced here: 37.2 us
  Pallas kernels  18.3 us (49%)
  starting transfers between devices  17.1 us (45%)
  waiting for transfers between devices  1.11 us (3%)
  between operations  0.72 us (2%)
    pallas_call x1, Pallas kernels, advect(): pl.pallas_call(functools.partial(advect_body, ny // EDGE, nz // EDGE), in...  8.35 us
    ppermute x4, starting transfers between devices, passed_around(): lax.ppermute(block, axis, [(i, (i + distance) % size) for i in range(size)])  7.78 us
    all_to_all x1, starting transfers between devices, per_device(): lax.all_to_all(sampled, 'member', split_axis=0, concat_axis=0, tiled=True)  5.92 us
    pallas_call x1, Pallas kernels, add_drag(): pl.pallas_call(functools.partial(source_body, ny // EDGE, nz // EDGE), in...  5.79 us
    all_to_all x1, starting transfers between devices, per_device(): lax.all_to_all(parcels, 'member', split_axis=0, concat_axis=0, tiled=True)  3.39 us
    pallas_call x1, Pallas kernels, pack(): pl.pallas_call(pack_body, in_specs=[pl.BlockSpec(memory_space=pltpu.HBM)]...  1.79 us
    pallas_call x1, Pallas kernels, sample_parcels(): pl.pallas_call(sample_body, in_specs=[pl.BlockSpec(memory_space=pltpu.VME...  1.67 us
    all_to_all x1, waiting for transfers between devices, per_device(): lax.all_to_all(sampled, 'member', split_axis=0, concat_axis=0, tiled=True)  1.09 us
  transfers between devices with their start and end apart: 6, of which 1 were waited for; matrix products, arithmetic and copies ran while one was open for 0% of the time, Pallas kernels for 38%

profile of v4, /device:TPU:0, one launch (start us, length us, event | category | flops | bytes accessed | tf_op | source)
XLA Modules:
  0.0 37.2 jit_solution(7106830092833734410)
XLA Ops:
  0.6 1.8 %pack.1 = (f32[8,6,2,512]{3,2,1,0:T(2,128)}, bf16[2,64,256]{2,1,0:T(8,128)(2,1)S(1)}, bf16[1,64,256]{2,1,0:T(8,128)(2,1)S(1)}, bf16[2,64,256]{2,1,0:T(8,128)(2,1)S(1)}, bf16[1,64,256]{2,1,0:T(8,128)(2,1)S(1)}) custom-call(f32[8,3,2,512]{3,2,1,0:T(2,128)} %bitcast.11, f32[8,2,512]{2,1,0:T(2,128)} %bitcast.13, f32[8,2,512]{2,1,0:T(2,128)} %bitcast.16, ...), custom_call_target="tpu_custom_call" | custom-call | tf_op jit(solution)/shard_map/pack/pallas_call | solution.py:83
  2.4 0.5 %collective-permute-start = (bf16[2,64,256]{2,1,0:T(8,128)(2,1)S(1)}, bf16[2,64,256]{2,1,0:T(8,128)(2,1)S(1)}, u32[]{:S(2)}, u32[]{:S(2)}) collective-permute-start(bf16[2,64,256]{2,1,0:T(8,128)(2,1)S(1)} %get-tuple-element.14), channel_id=1, source_target_pairs={{0,8},{8,16},{16,24},{24,0},{1,9},{9,17},{17,25},{25,1},{2,10},{10... | collective-permute-start | bytes 196616 | tf_op jit(solution)/shard_map/ppermute | solution.py:24
  2.9 2.6 %collective-permute-start.2 = (bf16[2,64,256]{2,1,0:T(8,128)(2,1)S(1)}, bf16[2,64,256]{2,1,0:T(8,128)(2,1)S(1)}, u32[]{:S(2)}, u32[]{:S(2)}) collective-permute-start(bf16[2,64,256]{2,1,0:T(8,128)(2,1)S(1)} %get-tuple-element.16), channel_id=1, source_target_pairs={{0,1},{1,2},{2,3},{3,4},{4,5},{5,6},{6,7},{7,0},{8,9},{9,10},{10,1... | collective-permute-start | bytes 196616 | tf_op jit(solution)/shard_map/ppermute | solution.py:24
  5.5 1.4 %collective-permute-start.1 = (bf16[1,64,256]{2,1,0:T(8,128)(2,1)S(1)}, bf16[1,64,256]{2,1,0:T(8,128)(2,1)S(1)}, u32[]{:S(2)}, u32[]{:S(2)}) collective-permute-start(bf16[1,64,256]{2,1,0:T(8,128)(2,1)S(1)} %get-tuple-element.15), channel_id=1, source_target_pairs={{0,24},{8,0},{16,8},{24,16},{1,25},{9,1},{17,9},{25,17},{2,26},{10... | collective-permute-start | bytes 98312 | tf_op jit(solution)/shard_map/ppermute | solution.py:24
  6.9 3.3 %collective-permute-start.3 = (bf16[1,64,256]{2,1,0:T(8,128)(2,1)S(1)}, bf16[1,64,256]{2,1,0:T(8,128)(2,1)S(1)}, u32[]{:S(2)}, u32[]{:S(2)}) collective-permute-start(bf16[1,64,256]{2,1,0:T(8,128)(2,1)S(1)} %get-tuple-element.17), channel_id=1, source_target_pairs={{0,7},{1,0},{2,1},{3,2},{4,3},{5,4},{6,5},{7,6},{8,15},{9,8},{10,9... | collective-permute-start | bytes 98312 | tf_op jit(solution)/shard_map/ppermute | solution.py:24
  10.2 3.4 %all-to-all-start = ((f32[8,6,2,512]{3,2,1,0:T(2,128)}), f32[8,6,2,512]{3,2,1,0:T(2,128)S(1)}, u32[]{:S(2)}, u32[]{:S(2)}) async-start(f32[8,6,2,512]{3,2,1,0:T(2,128)} %get-tuple-element.19), calls=%async_computation | async-start | bytes 393216 | tf_op jit(solution)/shard_map/all_to_all | solution.py:649
  13.6 0.0 collective-permute-done.1.halo_above_x
  13.6 0.0 collective-permute-done.3.halo_above_y
  13.6 0.0 collective-permute-done.halo_below_x
  13.6 0.0 collective-permute-done.2.halo_below_y
  13.6 8.4 %advect.1 = (f32[64,64,256]{2,1,0:T(8,128)}, bf16[16,64,256]{2,1,0:T(8,128)(2,1)S(1)}) custom-call(s32[16]{0:T(128)} %bitcast.18, s32[16]{0:T(128)} %bitcast.20, bf16[2,64,256]{2,1,0:T(8,128)(2,1)S(1)} %collective-permute-done.halo_below_x, bf16[1,64,256]{2,1,0:T(8,128)(2,1)S(1)} %collective-permute-done.1.halo_above_x, ...), custom_call_target="tpu_custom_call" | custom-call | flops 9093251072 | bytes 117440512 | tf_op jit(solution)/shard_map/advect/pallas_call | solution.py:370
  22.0 0.0 all-to-all-done.parcels_ref
  22.0 1.7 %sample.1 = (bf16[8,8,512]{2,1,0:T(8,128)(2,1)}, bf16[8,8,512]{2,1,0:T(8,128)(2,1)S(1)}) custom-call(f32[8,6,2,512]{3,2,1,0:T(2,128)S(1)} %all-to-all-done.parcels_ref, bf16[16,64,256]{2,1,0:T(8,128)(2,1)S(1)} %get-tuple-element.22.windows_ref), custom_call_target="tpu_custom_call" | custom-call | tf_op jit(solution)/shard_map/sample/pallas_call | solution.py:449
  23.7 5.9 %all-to-all-start.1 = ((bf16[8,8,512]{2,1,0:T(8,128)(2,1)}), bf16[8,8,512]{2,1,0:T(8,128)(2,1)S(1)}, u32[]{:S(2)}, u32[]{:S(2)}) async-start(bf16[8,8,512]{2,1,0:T(8,128)(2,1)} %get-tuple-element.24), calls=%async_computation.1 | async-start | bytes 131072 | tf_op jit(solution)/shard_map/all_to_all | solution.py:656
  29.6 0.0 copy-start
  29.6 0.0 copy-start.1
  29.6 5.8 %add_drag.1 = bf16[3,64,64,256]{3,2,1,0:T(8,128)(2,1)} custom-call(s32[16]{0:T(128)} %bitcast.19, s32[16]{0:T(128)} %bitcast.21, f32[8,6,2,512]{3,2,1,0:T(2,128)S(1)} %all-to-all-done.parcels_ref, bf16[8,8,512]{2,1,0:T(8,128)(2,1)S(1)} %get-tuple-element.23.sampled_ref, bf16[3,64,64,256]{3,2,1,0:T(8,128)(2,1)} %vel_hbm.3), custom_call_target="tpu_custom_call" | custom-call | tf_op jit(solution)/shard_map/add_drag/pallas_call | solution.py:590
  35.4 1.1 %all-to-all-done.1.sampled_ref = bf16[8,8,512]{2,1,0:T(8,128)(2,1)S(1)} async-done(((bf16[8,8,512]{2,1,0:T(8,128)(2,1)}), bf16[8,8,512]{2,1,0:T(8,128)(2,1)S(1)}, u32[]{:S(2)}, u32[]{:S(2)}) %all-to-all-start.1) | async-done | bytes 65568 | tf_op jit(solution)/shard_map/all_to_all | solution.py:656
  36.5 0.0 copy-done
  36.5 0.0 copy-done.1
  36.5 0.7 %drag.1 = f32[8,3,2,512]{3,2,1,0:T(2,128)} custom-call(f32[8,3,2,512]{3,2,1,0:T(2,128)S(1)} %bitcast.12, f32[8,2,512]{2,1,0:T(2,128)S(1)} %bitcast.14, bf16[8,8,512]{2,1,0:T(8,128)(2,1)S(1)} %all-to-all-done.1.sampled_ref), custom_call_target="tpu_custom_call" | custom-call | tf_op jit(solution)/shard_map/drag/pallas_call | solution.py:620
Async XLA Ops:
  2.4 11.2 %collective-permute-start = (bf16[2,64,256]{2,1,0:T(8,128)(2,1)S(1)}, bf16[2,64,256]{2,1,0:T(8,128)(2,1)S(1)}, u32[]{:S(2)}, u32[]{:S(2)}) collective-permute-start(bf16[2,64,256]{2,1,0:T(8,128)(2,1)S(1)} %get-tuple-element.14), channel_id=1, source_target_pairs={{0,8},{8,16},{16,24},{24,0},{1,9},{9,17},{17,25},{25,1},{2,10},{10... | collective-permute-start | bytes 196616 | tf_op jit(solution)/shard_map/ppermute | solution.py:24
  2.9 10.7 %collective-permute-start.2 = (bf16[2,64,256]{2,1,0:T(8,128)(2,1)S(1)}, bf16[2,64,256]{2,1,0:T(8,128)(2,1)S(1)}, u32[]{:S(2)}, u32[]{:S(2)}) collective-permute-start(bf16[2,64,256]{2,1,0:T(8,128)(2,1)S(1)} %get-tuple-element.16), channel_id=1, source_target_pairs={{0,1},{1,2},{2,3},{3,4},{4,5},{5,6},{6,7},{7,0},{8,9},{9,10},{10,1... | collective-permute-start | bytes 196616 | tf_op jit(solution)/shard_map/ppermute | solution.py:24
  5.5 8.1 %collective-permute-start.1 = (bf16[1,64,256]{2,1,0:T(8,128)(2,1)S(1)}, bf16[1,64,256]{2,1,0:T(8,128)(2,1)S(1)}, u32[]{:S(2)}, u32[]{:S(2)}) collective-permute-start(bf16[1,64,256]{2,1,0:T(8,128)(2,1)S(1)} %get-tuple-element.15), channel_id=1, source_target_pairs={{0,24},{8,0},{16,8},{24,16},{1,25},{9,1},{17,9},{25,17},{2,26},{10... | collective-permute-start | bytes 98312 | tf_op jit(solution)/shard_map/ppermute | solution.py:24
  6.9 6.7 %collective-permute-start.3 = (bf16[1,64,256]{2,1,0:T(8,128)(2,1)S(1)}, bf16[1,64,256]{2,1,0:T(8,128)(2,1)S(1)}, u32[]{:S(2)}, u32[]{:S(2)}) collective-permute-start(bf16[1,64,256]{2,1,0:T(8,128)(2,1)S(1)} %get-tuple-element.17), channel_id=1, source_target_pairs={{0,7},{1,0},{2,1},{3,2},{4,3},{5,4},{6,5},{7,6},{8,15},{9,8},{10,9... | collective-permute-start | bytes 98312 | tf_op jit(solution)/shard_map/ppermute | solution.py:24
  10.2 11.8 %all-to-all-start = ((f32[8,6,2,512]{3,2,1,0:T(2,128)}), f32[8,6,2,512]{3,2,1,0:T(2,128)S(1)}, u32[]{:S(2)}, u32[]{:S(2)}) async-start(f32[8,6,2,512]{3,2,1,0:T(2,128)} %get-tuple-element.19), calls=%async_computation | async-start | bytes 393216 | tf_op jit(solution)/shard_map/all_to_all | solution.py:649
  23.7 12.8 %all-to-all-start.1 = ((bf16[8,8,512]{2,1,0:T(8,128)(2,1)}), bf16[8,8,512]{2,1,0:T(8,128)(2,1)S(1)}, u32[]{:S(2)}, u32[]{:S(2)}) async-start(bf16[8,8,512]{2,1,0:T(8,128)(2,1)} %get-tuple-element.24), calls=%async_computation.1 | async-start | bytes 131072 | tf_op jit(solution)/shard_map/all_to_all | solution.py:656
  29.6 6.9 %copy-start = (f32[1,1,8,2,3,512]{5,3,4,2,1,0:T(2,128)S(1)}, f32[1,1,8,2,3,512]{5,3,4,2,1,0:T(2,128)}, u32[]{:S(2)}) copy-start(f32[1,1,8,2,3,512]{5,3,4,2,1,0:T(2,128)} %param.12) | copy-start | bytes 294916
  29.6 6.9 %copy-start.1 = (f32[1,1,8,2,512]{4,3,2,1,0:T(2,128)S(1)}, f32[1,1,8,2,512]{4,3,2,1,0:T(2,128)}, u32[]{:S(2)}) copy-start(f32[1,1,8,2,512]{4,3,2,1,0:T(2,128)} %param.13) | copy-start | bytes 98308
